TPU v7x, 512 devices: a whole 4x4x16 slice. The times are simulated.
512 devices in a mesh: dp: 64 (over z, y), mp: 8 (over x, core).
Axes of the slice: x: 4, y: 4, z: 16, core: 2. Of those that a mesh axis runs over, the one named last changes fastest.
Arguments:
- hidden_rows: bfloat16 [64, 384, 4096], P('dp'), may hold values from -6 to 6
- norm_gain: float32 [4096], replicated, may hold values from 0.5 to 1.5
- w_query: bfloat16 [4096, 2048], P('dp', 'mp'), may hold values from -0.01171875 to 0.01171875
- w_key: bfloat16 [4096, 2048], P('dp', 'mp'), may hold values from -0.09375 to 0.09375
- w_value: bfloat16 [4096, 2048], P('dp', 'mp'), may hold values from -0.09375 to 0.09375
- head_cotangent: bfloat16 [64, 484, 2048], P('dp', None, 'mp'), may hold values from -6 to 6
- prompt_cotangent: bfloat16 [64, 100, 4096], P('dp'), may hold values from -0.29882812 to 0.29882812
- prompt_master: float32 [100, 4096], P(None, 'dp'), may hold values from -5 to 5
- prompt_first: float32 [100, 4096], P(None, 'dp'), may hold values from -0.6 to 0.6
- prompt_second: float32 [100, 4096], P(None, 'dp'), may hold values from 0.01 to 1
- row_factor: float32 [4096, 100], P('dp'), may hold values from 0.5 to 1.5
- row_first: float32 [4096, 100], P('dp'), may hold values from -3 to 3
- row_second: float32 [4096, 100], P('dp'), may hold values from 0.1 to 10
- col_factor: float32 [4096, 4096], P('dp', 'mp'), may hold values from 0.5 to 1.5
- col_first: float32 [4096, 4096], P('dp', 'mp'), may hold values from -0.6 to 0.6
- col_second: float32 [4096, 4096], P('dp', 'mp'), may hold values from 0.01 to 1
- row_tenant: int32 [64], P('dp'), may hold values from 0 to 4095
- tenant_slot: int32 [4096], replicated, may hold values from 0 to 4095, each once
Outputs:
- prompt_out: float32 [100, 4096], P(None, 'dp')
- prompt_first_out: float32 [100, 4096], P(None, 'dp')
- prompt_second_out: float32 [100, 4096], P(None, 'dp')
- row_out: float32 [4096, 100], P('dp')
- row_first_out: float32 [4096, 100], P('dp')
- row_second_out: float32 [4096, 100], P('dp')
- col_out: float32 [4096, 4096], P('dp', 'mp')
- col_first_out: float32 [4096, 4096], P('dp', 'mp')
- col_second_out: float32 [4096, 4096], P('dp', 'mp')
Inputs may be any that keep to these rules, and one draw needn't show every extreme that they name: `row_tenant`: each row's tenant. `tenant_slot`: each tenant has one slot, each slot one tenant; slot s is held by dp index s // 64.
All inputs are finite; a program needn't handle non-finite values.
Results may differ from a plain program's by a relative error of at most 0.0073.
Values may be sent and summed in bfloat16 or wider, within the bound.
No kernel may reach another device: no remote copies, remote signals or barrier semaphores. Data moves between devices by JAX's collectives and lax.ppermute only.
A program may use at most 64 MiB of HBM per device.

v0:
```python
import jax
import jax.numpy as jnp
from jax import lax
from jax.sharding import PartitionSpec as P

HEAD_DIM = 64
PROMPT = 100


beta_first = 0.9
beta_second = 0.99
learn_rate = 0.01
adam_epsilon = 1e-08
norm_epsilon = 1e-06


def adam_step(param, moment_one, moment_two, gradient):
    first_new = beta_first * moment_one + (1.0 - beta_first) * gradient
    second_new = beta_second * moment_two + (1.0 - beta_second) * gradient * gradient
    return (
        param - learn_rate * first_new / (jnp.sqrt(second_new) + adam_epsilon),
        first_new,
        second_new,
    )


def local(
    hidden_rows,
    norm_gain,
    w_query,
    w_key,
    w_value,
    head_cotangent,
    prompt_cotangent,
    prompt_master,
    prompt_first,
    prompt_second,
    row_factor,
    row_first,
    row_second,
    col_factor,
    col_first,
    col_second,
    row_tenant,
    tenant_slot,
):
    group_size = lax.axis_size("dp")
    device = lax.axis_index("dp")
    owned_count = row_factor.shape[0]
    col_width = col_factor.shape[1]
    col_start = lax.axis_index("mp") * col_width
    all_tenants = lax.all_gather(row_tenant, "dp", axis=0, tiled=True)
    catalog = lax.broadcasted_iota(jnp.int32, (group_size, tenant_slot.shape[0]), 1)
    slot_ids = jnp.sum(jnp.where(catalog == all_tenants[:, None], tenant_slot[None, :], 0), axis=1)
    local_slot = slot_ids - device * owned_count
    picker = (
        local_slot[:, None] == lax.broadcasted_iota(jnp.int32, (group_size, owned_count), 1)
    ).astype(jnp.float32)
    row_term = jnp.dot(picker, row_factor, precision=lax.Precision.HIGHEST)
    col_term = jnp.dot(picker, col_factor, precision=lax.Precision.HIGHEST)
    row_all, col_all = lax.psum((row_term, col_term), "dp")
    factor_rows = lax.dynamic_index_in_dim(row_all, device, 0, keepdims=False)
    my_cols = lax.dynamic_index_in_dim(col_all, device, 0, keepdims=False)
    factor_cols = lax.all_gather(my_cols, "mp", axis=0, tiled=True)
    prompt_base = lax.all_gather(prompt_master.astype(jnp.bfloat16), "dp", axis=1, tiled=True)
    query_full, key_full, value_full = (
        lax.all_gather(w_query, "dp", axis=0, tiled=True),
        lax.all_gather(w_key, "dp", axis=0, tiled=True),
        lax.all_gather(w_value, "dp", axis=0, tiled=True),
    )
    base_float = prompt_base.astype(jnp.float32)
    prompt_act = (base_float * factor_rows[:, None] * factor_cols[None, :]).astype(jnp.bfloat16)
    stacked = jnp.concatenate([prompt_act, hidden_rows[0]], axis=0)
    floated = stacked.astype(jnp.float32)
    inverse = lax.rsqrt(jnp.mean(floated * floated, axis=-1, keepdims=True) + norm_epsilon)
    unit_rows = floated * inverse
    normed = (unit_rows * norm_gain[None, :]).astype(jnp.bfloat16)
    length = stacked.shape[0]
    inner_local = query_full.shape[1]
    heads_local = inner_local // HEAD_DIM
    queries = (
        jnp.dot(normed, query_full, preferred_element_type=jnp.float32)
        .astype(jnp.bfloat16)
        .reshape(length, heads_local, HEAD_DIM)
    )
    keyset = (
        jnp.dot(normed, key_full, preferred_element_type=jnp.float32)
        .astype(jnp.bfloat16)
        .reshape(length, heads_local, HEAD_DIM)
    )
    valueset = (
        jnp.dot(normed, value_full, preferred_element_type=jnp.float32)
        .astype(jnp.bfloat16)
        .reshape(length, heads_local, HEAD_DIM)
    )
    upstream = head_cotangent[0].reshape(length, heads_local, HEAD_DIM)
    scores = jnp.einsum("qhd,khd->hqk", queries, keyset, preferred_element_type=jnp.float32)
    exponent = jnp.exp(scores)
    attend = exponent / jnp.sum(exponent, axis=-1, keepdims=True)
    attend_low = attend.astype(jnp.bfloat16)
    grad_prob = jnp.einsum("qhd,khd->hqk", upstream, valueset, preferred_element_type=jnp.float32)
    row_dot = jnp.sum(attend * grad_prob, axis=-1, keepdims=True)
    grad_score = (attend * (grad_prob - row_dot)).astype(jnp.bfloat16)
    grad_query = jnp.einsum(
        "hqk,khd->qhd", grad_score[:, :PROMPT, :], keyset, preferred_element_type=jnp.float32
    ).astype(jnp.bfloat16)
    grad_key = jnp.einsum(
        "hqk,qhd->khd", grad_score[:, :, :PROMPT], queries, preferred_element_type=jnp.float32
    ).astype(jnp.bfloat16)
    grad_value = jnp.einsum(
        "hqk,qhd->khd", attend_low[:, :, :PROMPT], upstream, preferred_element_type=jnp.float32
    ).astype(jnp.bfloat16)
    contract = (((1,), (1,)), ((), ()))
    head_part = lax.dot_general(
        grad_query.reshape(PROMPT, inner_local),
        query_full,
        contract,
        preferred_element_type=jnp.float32,
    )
    head_part = head_part + lax.dot_general(
        grad_key.reshape(PROMPT, inner_local),
        key_full,
        contract,
        preferred_element_type=jnp.float32,
    )
    head_part = head_part + lax.dot_general(
        grad_value.reshape(PROMPT, inner_local),
        value_full,
        contract,
        preferred_element_type=jnp.float32,
    )
    unit_prompt = unit_rows[:PROMPT]
    inverse_prompt = inverse[:PROMPT]
    head_total = lax.psum(head_part, "mp")
    scaled = head_total * norm_gain[None, :]
    grad_norm = inverse_prompt * (
        scaled - unit_prompt * jnp.mean(scaled * unit_prompt, axis=-1, keepdims=True)
    )
    grad_prompt = prompt_cotangent[0].astype(jnp.float32) + grad_norm
    grad_rows = jnp.sum(grad_prompt * base_float * factor_cols[None, :], axis=-1)
    grad_cols = jnp.sum(grad_prompt * base_float * factor_rows[:, None], axis=0)
    grad_base = grad_prompt * factor_rows[:, None] * factor_cols[None, :]
    col_slice = lax.dynamic_slice_in_dim(grad_cols, col_start, col_width, 0)
    reduced = lax.psum_scatter(grad_base, "dp", scatter_dimension=1, tiled=True)
    rows_all, cols_all = (
        lax.all_gather(grad_rows[None, :], "dp", axis=0, tiled=True),
        lax.all_gather(col_slice[None, :], "dp", axis=0, tiled=True),
    )
    owner_contract = (((0,), (0,)), ((), ()))
    row_grad = lax.dot_general(picker, rows_all, owner_contract, precision=lax.Precision.HIGHEST)
    col_grad = lax.dot_general(picker, cols_all, owner_contract, precision=lax.Precision.HIGHEST)
    prompt_out, prompt_first_out, prompt_second_out = adam_step(
        prompt_master, prompt_first, prompt_second, reduced
    )
    row_out, row_first_out, row_second_out = adam_step(row_factor, row_first, row_second, row_grad)
    col_out, col_first_out, col_second_out = adam_step(col_factor, col_first, col_second, col_grad)
    return (
        prompt_out,
        prompt_first_out,
        prompt_second_out,
        row_out,
        row_first_out,
        row_second_out,
        col_out,
        col_first_out,
        col_second_out,
    )


def solution(mesh):
    return jax.shard_map(
        local,
        mesh=mesh,
        in_specs=(
            P("dp", None, None),
            P(),
            P("dp", "mp"),
            P("dp", "mp"),
            P("dp", "mp"),
            P("dp", None, "mp"),
            P("dp", None, None),
            P(None, "dp"),
            P(None, "dp"),
            P(None, "dp"),
            P("dp", None),
            P("dp", None),
            P("dp", None),
            P("dp", "mp"),
            P("dp", "mp"),
            P("dp", "mp"),
            P("dp"),
            P(),
        ),
        out_specs=(
            P(None, "dp"),
            P(None, "dp"),
            P(None, "dp"),
            P("dp", None),
            P("dp", None),
            P("dp", None),
            P("dp", "mp"),
            P("dp", "mp"),
            P("dp", "mp"),
        ),
        check_vma=False,
    )
```

profile of v0, /device:TPU:1, one launch (start us, length us, event | category | flops | bytes accessed | tf_op | source)
XLA Modules:
  0.0 1523.6 jit_solution(12534171961508251864)
XLA Ops:
  10.2 29.8 %all-reduce = s32[64]{0:T(128)S(1)} all-reduce(s32[64]{0:T(128)S(1)} %dynamic-update-slice), channel_id=1, replica_groups=mesh['dp'=64,'mp'=8] {'dp'}, use_global_device_ids=true, to_apply=%add | all-reduce | flops 64 | bytes 512
  40.9 1.8 fusion.18
  45.7 84.1 %all_gather.24 = bf16[100,4096]{0,1:T(8,128)(2,1)} all-gather(bf16[100,64]{0,1:T(8,128)(2,1)S(1)} %convert_element_type.57), channel_id=1, replica_groups=mesh['dp'=64,'mp'=8] {'dp'}, dimensions={1}, use_global_device_ids=true | all-gather | bytes 832000 | tf_op jit(solution)/shard_map/all_gather | solution.py:65
  129.8 2.4 copy.67
  133.5 221.2 %psum.21 = f32[64,100]{1,0:T(8,128)S(1)} all-reduce(f32[64,100]{1,0:T(8,128)S(1)} %fusion.19), channel_id=1, replica_groups=mesh['dp'=64,'mp'=8] {'dp'}, use_global_device_ids=true, to_apply=%region_1.2 | all-reduce | flops 6400 | bytes 51200 | tf_op jit(solution)/shard_map/psum | solution.py:61
  355.4 96.7 %all-gather = f32[1,4096]{1,0:T(1,128)S(1)} all-gather(f32[1,512]{1,0:T(1,128)S(1)} %constant_dynamic-slice_fusion), channel_id=2, replica_groups=mesh['dp'=64,'mp'=8] {'mp'}, dimensions={1}, use_global_device_ids=true | all-gather | bytes 18432 | tf_op jit(solution)/shard_map/all_gather | solution.py:64
  456.1 4.2 convolution_convert_fusion.2
  462.1 109.8 %all-gather.10.cloned.1.call-done = bf16[4096,256]{1,0:T(8,128)(2,1)} async-done(((bf16[64,256]{1,0:T(8,128)(2,1)}), bf16[4096,256]{1,0:T(8,128)(2,1)}) %all-gather.10.cloned.1.call-update) | async-done | bytes 2097168 | tf_op jit(solution)/shard_map/all_gather | solution.py:67
  571.9 4.2 convolution_convert_fusion.1
  577.8 133.9 %all-gather.12.cloned.1.call-done = bf16[4096,256]{1,0:T(8,128)(2,1)} async-done(((bf16[64,256]{1,0:T(8,128)(2,1)}), bf16[4096,256]{1,0:T(8,128)(2,1)}) %all-gather.12.cloned.1.call-update) | async-done | bytes 2097168 | tf_op jit(solution)/shard_map/all_gather | solution.py:69
  711.7 4.2 convolution_convert_fusion
  717.6 1.8 exponential_reduce_fusion
  719.4 2.4 exponential_divide_fusion
  721.9 6.0 fusion.3
  732.1 2.4 fusion.27
  736.1 2.0 convolution_add_fusion
  738.4 5.5 convert_multiply_fusion
  743.9 77.3 %all-reduce.7.cloned.1.call-done = f32[100,4096]{1,0:T(8,128)} async-done(((f32[100,4096]{1,0:T(8,128)}), f32[100,4096]{1,0:T(8,128)}) %all-reduce.7.cloned.1.call-update) | async-done | bytes 1638416 | tf_op jit(solution)/shard_map/psum | solution.py:134
  821.2 2.4 multiply_reduce_fusion.2
  823.7 2.5 multiply_reduce_fusion
  826.6 1.9 copy.79
  829.8 225.0 %all-reduce.1 = f32[6400]{0:T(1024)S(1)} all-reduce(f32[6400]{0:T(1024)S(1)} %dynamic-update-slice.1), channel_id=3, replica_groups=mesh['dp'=64,'mp'=8] {'dp'}, use_global_device_ids=true, to_apply=%add.1 | all-reduce | flops 6400 | bytes 51200
  1055.0 73.0 %all-gather.3 = f32[64,1,512]{2,1,0:T(1,128)S(1)} all-gather(f32[1,1,512]{2,1,0:T(1,128)S(1)} %bitcast.82), channel_id=4, replica_groups=mesh['dp'=64,'mp'=8] {'dp'}, dimensions={0}, use_global_device_ids=true | all-gather | bytes 133120 | tf_op jit(solution)/shard_map/all_gather | solution.py:147
  1130.0 383.7 %reduce-scatter.4.cloned.1.call-done = f32[64,100]{1,0:T(8,128)} async-done(((f32[4096,100]{1,0:T(8,128)}), f32[64,100]{1,0:T(8,128)}) %reduce-scatter.4.cloned.1.call-update) | async-done | bytes 25616
  (88 shorter events, 29.8 us)
Async XLA Ops:
  7.2 126.1 %copy-start.10 = (f32[64,100]{1,0:T(8,128)S(1)}, f32[64,100]{1,0:T(8,128)}, u32[]{:S(2)}) copy-start(f32[64,100]{1,0:T(8,128)} %param.28) | copy-start | bytes 76804
  7.2 447.3 %copy-start = (bf16[1,384,4096]{2,1,0:T(8,128)(2,1)S(1)}, bf16[1,384,4096]{2,1,0:T(8,128)(2,1)}, u32[]{:S(2)}) copy-start(bf16[1,384,4096]{2,1,0:T(8,128)(2,1)} %param.18) | copy-start | bytes 9437188
  7.2 347.5 %all-reduce.5.cloned.1.call-start = ((), (), s32[]{:S(2)}) async-start(), calls=%async_computation.1 | async-start | bytes 262144 | tf_op jit(solution)/shard_map/psum | solution.py:61
  42.8 413.3 %all-gather.8.cloned.1.call-start = ((), (), s32[]{:S(2)}) async-start(), calls=%async_computation.2 | async-start | bytes 2129920 | tf_op jit(solution)/shard_map/all_gather | solution.py:68
  43.5 528.3 %all-gather.10.cloned.1.call-start = ((), (), s32[]{:S(2)}) async-start(), calls=%async_computation.3 | async-start | bytes 2129920 | tf_op jit(solution)/shard_map/all_gather | solution.py:67
  44.3 667.4 %all-gather.12.cloned.1.call-start = ((), (), s32[]{:S(2)}) async-start(), calls=%async_computation.4 | async-start | bytes 2129920 | tf_op jit(solution)/shard_map/all_gather | solution.py:69
  44.8 776.4 %all-reduce.7.cloned.1.call-start = ((), (), s32[]{:S(2)}) async-start(), calls=%async_computation.5 | async-start | bytes 3407872 | tf_op jit(solution)/shard_map/psum | solution.py:134
  132.1 324.0 %copy-start.12 = (f32[4096]{0:T(1024)S(1)}, f32[4096]{0:T(1024)}, u32[]{:S(2)}) copy-start(f32[4096]{0:T(1024)} %param.19) | copy-start | bytes 49156
  456.1 282.3 %copy-start.17 = (f32[484]{0:T(512)}, f32[484]{0:T(512)S(1)}, u32[]{:S(2)}) copy-start(f32[484]{0:T(512)S(1)} %add_rsqrt_fusion) | copy-start | bytes 5812
  727.8 6.7 copy-start.4
  734.5 1.6 copy-start.5
  738.1 775.6 %reduce-scatter.4.cloned.1.call-start = ((), (), s32[]{:S(2)}) async-start(), calls=%async_computation.6 | async-start | bytes 2129920
  743.9 79.7 %copy-start.2 = (bf16[100,4096]{1,0:T(8,128)(2,1)S(1)}, bf16[100,4096]{1,0:T(8,128)(2,1)}, u32[]{:S(2)}) copy-start(bf16[100,4096]{1,0:T(8,128)(2,1)} %copy.67) | copy-start | bytes 2457604
  743.9 79.8 %copy-start.6 = (bf16[1,100,4096]{2,1,0:T(8,128)(2,1)S(1)}, bf16[1,100,4096]{2,1,0:T(8,128)(2,1)}, u32[]{:S(2)}) copy-start(bf16[1,100,4096]{2,1,0:T(8,128)(2,1)} %param.24) | copy-start | bytes 2457604
  743.9 79.8 %slice-start = ((f32[484]{0:T(512)}), f32[100]{0:T(128)S(1)}, s32[]{:S(2)}) async-start(f32[484]{0:T(512)} %copy-done.17), calls=%async_computation.7 | async-start | bytes 1024 | tf_op jit(solution)/shard_map/slice | solution.py:133
  821.2 2.5 copy-start.3
  826.5 2.0 copy-start.11
  826.5 2.1 copy-start.15
  826.5 2.2 copy-start.16
  826.5 301.4 %copy-start.13 = (f32[64,100]{1,0:T(8,128)S(1)}, f32[64,100]{1,0:T(8,128)}, u32[]{:S(2)}) copy-start(f32[64,100]{1,0:T(8,128)} %param.29) | copy-start | bytes 76804
  826.5 301.4 %copy-start.14 = (f32[64,100]{1,0:T(8,128)S(1)}, f32[64,100]{1,0:T(8,128)}, u32[]{:S(2)}) copy-start(f32[64,100]{1,0:T(8,128)} %param.30) | copy-start | bytes 76804
  826.6 302.3 %copy-start.7 = (f32[64,512]{1,0:T(8,128)S(1)}, f32[64,512]{1,0:T(8,128)}, u32[]{:S(2)}) copy-start(f32[64,512]{1,0:T(8,128)} %param.31) | copy-start | bytes 393220
  826.6 302.3 %copy-start.8 = (f32[64,512]{1,0:T(8,128)S(1)}, f32[64,512]{1,0:T(8,128)}, u32[]{:S(2)}) copy-start(f32[64,512]{1,0:T(8,128)} %param.32) | copy-start | bytes 393220
  826.6 302.3 %copy-start.9 = (f32[64,512]{1,0:T(8,128)S(1)}, f32[64,512]{1,0:T(8,128)}, u32[]{:S(2)}) copy-start(f32[64,512]{1,0:T(8,128)} %param.33) | copy-start | bytes 393220
  (1 other events, 0.9 us)
Sparse Core Ops, SparseCore 0:
  42.9 249.8 all-reduce.4
  295.8 136.7 all-gather.7
  435.5 136.2 all-gather.9
  574.7 136.9 all-gather.11
  738.2 82.9 all-reduce.6
  828.6 685.0 reduce-scatter.3
where the time goes:
time: 1530 us; the launch traced here: 1520 us
  blocking collectives  730 us (48%)
  waiting for transfers between devices  707 us (46%)
  matrix products  33.7 us (2%)
  local copies, waits for them, and re-layouts  19.1 us (1%)
  other arithmetic  18 us (1%)
  between operations  15.9 us (1%)
    unnamed x7, waiting for transfers between devices  386 us
    unnamed x2, blocking collectives  255 us
    psum x1, blocking collectives, local(): row_all, col_all = lax.psum((row_term, col_term), 'dp')  221 us
    all_gather x1, waiting for transfers between devices, local(): lax.all_gather(w_value, 'dp', axis=0, tiled=True)  134 us
    all_gather x1, waiting for transfers between devices, local(): lax.all_gather(w_query, 'dp', axis=0, tiled=True)  110 us
    all_gather x1, blocking collectives, local(): factor_cols = lax.all_gather(my_cols, 'mp', axis=0, tiled=True)  96.7 us
    all_gather x1, blocking collectives, local(): lax.all_gather(prompt_master.astype(jnp.bfloat16), 'dp', axis=1, tiled=True)  84.1 us
    psum x1, waiting for transfers between devices, local(): head_total = lax.psum(head_part, 'mp')  77.3 us
  transfers between devices with their start and end apart: 6, of which 4 were waited for; matrix products, arithmetic and copies ran while one was open for 2% of the time, Pallas kernels for 0%

commit v1 on v0

v1 whole, which is shorter than its diff:
```python
import jax
import jax.numpy as jnp
from jax import lax
from jax.experimental import pallas as pl
from jax.experimental.pallas import tpu as pltpu
from jax.sharding import Mesh, PartitionSpec as P

HEAD_DIM = 64
PROMPT = 100
PAD = 128
BLOCK = 16
LANES = 128

beta_first = 0.9
beta_second = 0.99
learn_rate = 0.01
adam_epsilon = 1e-08
norm_epsilon = 1e-06

ROWS_AXES = ("z", "y")
HEADS_AXES = ("x", "c")
BF16 = jnp.bfloat16
F32 = jnp.float32
VMEM_LIMIT = 48 * 1024 * 1024


def adam_step(param, moment_one, moment_two, gradient):
    first_new = beta_first * moment_one + (1.0 - beta_first) * gradient
    second_new = beta_second * moment_two + (1.0 - beta_second) * gradient * gradient
    return (
        param - learn_rate * first_new / (jnp.sqrt(second_new) + adam_epsilon),
        first_new,
        second_new,
    )


def dot(a, b, da, db):
    return lax.dot_general(a, b, (((da,), (db,)), ((), ())), preferred_element_type=F32)


def attention_kernel(qkv_ref, up_ref, grads_ref, along_ref):
    length = up_ref.shape[0]
    inner = up_ref.shape[1]
    column = lax.broadcasted_iota(jnp.int32, (length, length), 1)
    real_key = (column < PROMPT) | (column >= PAD)
    along = jnp.zeros((PAD, 1), F32)
    for head in range(inner // HEAD_DIM):
        at = head * HEAD_DIM
        query = qkv_ref[:, at : at + HEAD_DIM]
        key = qkv_ref[:, inner + at : inner + at + HEAD_DIM]
        value = qkv_ref[:, 2 * inner + at : 2 * inner + at + HEAD_DIM]
        up = up_ref[:, at : at + HEAD_DIM]
        exponent = jnp.where(real_key, jnp.exp(dot(query, key, 1, 1)), 0.0)
        attend = exponent / jnp.sum(exponent, axis=1, keepdims=True)
        grad_prob = dot(up, value, 1, 1)
        row_dot = jnp.sum(attend * grad_prob, axis=1, keepdims=True)
        grad_score = (attend * (grad_prob - row_dot)).astype(BF16)
        grad_query = dot(grad_score[:PAD, :], key, 1, 0).astype(BF16)
        grad_key = dot(grad_score[:, :PAD], query, 0, 0).astype(BF16)
        grad_value = dot(attend[:, :PAD].astype(BF16), up, 0, 0).astype(BF16)
        for place, (grad, low) in enumerate(
            ((grad_query, query), (grad_key, key), (grad_value, value))
        ):
            grads_ref[:, place * inner + at : place * inner + at + HEAD_DIM] = grad
            along = along + jnp.sum(
                grad.astype(F32) * low[:PAD].astype(F32), axis=1, keepdims=True
            )
    along_ref[...] = jnp.broadcast_to(along, along_ref.shape)


def attention(qkv, up):
    return pl.pallas_call(
        attention_kernel,
        out_shape=(
            jax.ShapeDtypeStruct((PAD, qkv.shape[1]), BF16),
            jax.ShapeDtypeStruct((PAD, LANES), F32),
        ),
        in_specs=[pl.BlockSpec(memory_space=pltpu.VMEM)] * 2,
        out_specs=(pl.BlockSpec(memory_space=pltpu.VMEM),) * 2,
        compiler_params=pltpu.CompilerParams(vmem_limit_bytes=VMEM_LIMIT),
    )(qkv, up)


def head_kernel(
    width, grads_ref, weight_ref, along_ref, act_ref, base_ref, cot_ref, gain_ref, scale_ref, out_ref
):
    step = pl.program_id(0)
    part = dot(grads_ref[...], weight_ref[...], 1, 1)
    inverse = scale_ref[:, 0:1]
    rows = scale_ref[:, 1:2]
    mine = scale_ref[:, 2:3]
    mean = along_ref[:, 0:1] * (1.0 / width)
    unit = act_ref[...].astype(F32) * inverse
    grad = inverse * (part * gain_ref[...] - unit * mean) + mine * cot_ref[...].astype(F32)
    cols = jnp.sum(grad * base_ref[...].astype(F32) * rows, axis=0, keepdims=True)
    size = part.shape[1]
    out_ref[:, pl.ds(pl.multiple_of(step * size, size), size)] = part.astype(BF16)
    high = cols.astype(BF16).astype(F32)
    low = cols - high
    pieces = [high[:, at : at + LANES] for at in range(0, size, LANES)]
    pieces += [low[:, at : at + LANES] for at in range(0, size, LANES)]
    spare = BLOCK - len(pieces)
    if spare:
        pieces.append(jnp.zeros((spare, LANES), F32))
    out_ref[pl.ds(pl.multiple_of(step * BLOCK, BLOCK), BLOCK), width:] = jnp.concatenate(
        pieces, axis=0
    ).astype(BF16)


def head_parts(grads, weights, along, act, base, cot, gain, scale, groups):
    width = act.shape[1]
    size = width // groups
    full = lambda shape: pl.BlockSpec(shape, lambda i: (0,) * len(shape))
    stripe = lambda rows: pl.BlockSpec((rows, size), lambda i: (0, i))
    return pl.pallas_call(
        lambda *refs: head_kernel(width, *refs),
        grid=(groups,),
        out_shape=jax.ShapeDtypeStruct((PAD, width + LANES), BF16),
        in_specs=[
            full(grads.shape),
            pl.BlockSpec((size, weights.shape[1]), lambda i: (i, 0)),
            full(along.shape),
            stripe(PAD),
            stripe(PAD),
            stripe(PAD),
            stripe(1),
            full(scale.shape),
        ],
        out_specs=full((PAD, width + LANES)),
        compiler_params=pltpu.CompilerParams(vmem_limit_bytes=VMEM_LIMIT),
    )(grads, weights, along, act, base, cot, gain, scale)


def prompt_kernel(pieces, got_ref, act_ref, base_ref, cot_ref, gain_ref, cols_ref, scale_ref, out_ref):
    width = act_ref.shape[1]
    total = got_ref[0, :, :].astype(F32)
    for source in range(1, got_ref.shape[0]):
        total = total + got_ref[source, :, :].astype(F32)
    inverse = scale_ref[:, 0:1]
    rows = scale_ref[:, 1:2]
    unit = act_ref[...].astype(F32) * inverse
    scaled = total[:, :width] * gain_ref[...]
    mean = jnp.sum(scaled * unit, axis=1, keepdims=True) * (1.0 / width)
    grad = cot_ref[...].astype(F32) + inverse * (scaled - unit * mean)
    times_cols = grad * cols_ref[...]
    grad_rows = jnp.sum(times_cols * base_ref[...].astype(F32), axis=1, keepdims=True)
    grad_base = times_cols * rows
    extra = total[:, width:]
    cols = extra[:pieces, :] + extra[pieces : 2 * pieces, :]
    half = LANES // 2
    swapped = jnp.concatenate([cols[:, half:], cols[:, :half]], axis=1)
    spare = BLOCK - 2 * pieces
    lane = lax.broadcasted_iota(jnp.int32, (spare, LANES), 1)
    index = lax.broadcasted_iota(jnp.int32, (BLOCK, LANES), 0)
    line = jnp.sum(
        jnp.where(
            lax.broadcasted_iota(jnp.int32, (BLOCK, LANES), 1) == index + half, grad_rows, 0.0
        ),
        axis=0,
        keepdims=True,
    )
    under = jnp.where(lax.broadcasted_iota(jnp.int32, (spare, LANES), 0) == 0, line, 0.0)
    tail = jnp.concatenate([cols, swapped, under], axis=0)
    first_half = lax.broadcasted_iota(jnp.int32, (BLOCK, LANES), 1) < half
    for pair in range(width // LANES):
        block = grad_base[:, pair * LANES : (pair + 1) * LANES]
        other = jnp.concatenate([block[:, half:], block[:, :half]], axis=1)
        out_ref[2 * pair, :, :] = jnp.where(first_half, block, tail).astype(BF16)
        out_ref[2 * pair + 1, :, :] = jnp.where(first_half, other, tail).astype(BF16)


def prompt_grads(got, act, base, cot, gain, cols, scale, group_size, pieces):
    return pl.pallas_call(
        lambda *refs: prompt_kernel(pieces, *refs),
        out_shape=jax.ShapeDtypeStruct((group_size, BLOCK, LANES), BF16),
        in_specs=[pl.BlockSpec(memory_space=pltpu.VMEM)] * 7,
        out_specs=pl.BlockSpec(memory_space=pltpu.VMEM),
        compiler_params=pltpu.CompilerParams(vmem_limit_bytes=VMEM_LIMIT),
    )(got, act, base, cot, gain, cols, scale)


def local(
    hidden_rows,
    norm_gain,
    w_query,
    w_key,
    w_value,
    head_cotangent,
    prompt_cotangent,
    prompt_master,
    prompt_first,
    prompt_second,
    row_factor,
    row_first,
    row_second,
    col_factor,
    col_first,
    col_second,
    row_tenant,
    tenant_slot,
):
    dp, mp = ROWS_AXES, HEADS_AXES
    group_size = lax.axis_size(dp)
    groups = lax.axis_size(mp)
    device = lax.axis_index(dp)
    member = lax.axis_index(mp)
    owned_count = row_factor.shape[0]
    col_width = col_factor.shape[1]
    width = hidden_rows.shape[2]
    own_cols = prompt_master.shape[1]
    half = LANES // 2
    pieces = col_width // LANES

    weights = jnp.concatenate([w_query, w_key, w_value], axis=1)
    weights_y = lax.all_gather(weights, "y", axis=0, tiled=True)

    slot = lax.dynamic_index_in_dim(tenant_slot, row_tenant[0], 0, keepdims=False)
    base_own = jnp.pad(prompt_master.astype(BF16), ((0, PAD - PROMPT), (0, 0)))
    base_block = lax.dynamic_slice_in_dim(base_own, member * BLOCK, BLOCK, 0)
    marks = jnp.stack([slot // owned_count, slot % owned_count]).astype(BF16)
    marks = jnp.pad(jnp.broadcast_to(marks[None, :], (BLOCK, 2)), ((0, 0), (0, half - 2)))
    sent = jnp.concatenate([base_block, marks], axis=1)
    sent, weights_y = lax.optimization_barrier((sent, weights_y))
    weights_all = lax.all_gather(weights_y, "z", axis=0, tiled=True)
    got = lax.all_to_all(
        jnp.broadcast_to(sent[None], (group_size, BLOCK, LANES)), dp, 0, 0, tiled=False
    )
    base_mine = jnp.transpose(got[:, :, :own_cols], (1, 0, 2)).reshape(BLOCK, width)
    base = lax.all_to_all(
        jnp.broadcast_to(base_mine[None], (groups, BLOCK, width)), mp, 0, 0, tiled=False
    ).reshape(PAD, width)
    owner_all = got[:, 0, half].astype(jnp.int32)
    place_all = got[:, 0, half + 1].astype(jnp.int32)
    picker = (
        (owner_all == device)[:, None]
        & (place_all[:, None] == lax.broadcasted_iota(jnp.int32, (group_size, owned_count), 1))
    ).astype(F32)

    row_term = jnp.dot(picker, row_factor, precision=lax.Precision.HIGHEST)
    col_term = jnp.dot(picker, col_factor, precision=lax.Precision.HIGHEST)
    terms = jnp.concatenate(
        [
            col_term.reshape(group_size, pieces, LANES),
            jnp.pad(row_term, ((0, 0), (0, LANES - PROMPT)))[:, None, :],
            jnp.zeros((group_size, 8 - pieces - 1, LANES), F32),
        ],
        axis=1,
    )
    terms = jnp.sum(lax.all_to_all(terms, dp, 0, 0, tiled=False), axis=0)
    factor_rows = terms[pieces]
    my_cols = terms[:pieces].reshape(col_width)
    factor_cols = lax.all_gather(my_cols, mp, axis=0, tiled=True)

    gain = norm_gain[None, :]
    hidden = hidden_rows[0].astype(F32)
    hidden_inverse = lax.rsqrt(jnp.mean(hidden * hidden, axis=-1, keepdims=True) + norm_epsilon)
    hidden_normed = (hidden * hidden_inverse * gain).astype(BF16)
    act = (base.astype(F32) * factor_rows[:, None] * factor_cols[None, :]).astype(BF16)
    act_float = act.astype(F32)
    inverse = lax.rsqrt(jnp.mean(act_float * act_float, axis=-1, keepdims=True) + norm_epsilon)
    prompt_normed = (act_float * inverse * gain).astype(BF16)
    normed = jnp.concatenate([prompt_normed, hidden_normed], axis=0)
    qkv = jnp.dot(normed, weights_all, preferred_element_type=F32).astype(BF16)
    upstream = jnp.concatenate(
        [
            jnp.pad(head_cotangent[0, :PROMPT], ((0, PAD - PROMPT), (0, 0))),
            head_cotangent[0, PROMPT:],
        ],
        axis=0,
    )
    grads, along = attention(qkv, upstream)

    cot = jnp.pad(prompt_cotangent[0], ((0, PAD - PROMPT), (0, 0)))
    mine = (lax.broadcasted_iota(jnp.int32, (PAD, 1), 0) // BLOCK == member).astype(F32)
    scale = jnp.concatenate(
        [inverse, factor_rows[:, None], mine, jnp.zeros((PAD, LANES - 3), F32)], axis=1
    )
    parts = head_parts(grads, weights_all, along, act, base, cot, gain, scale, groups)
    parts = lax.all_to_all(
        parts.reshape(groups, BLOCK, width + LANES), mp, 0, 0, tiled=False
    )
    block = lambda array: lax.dynamic_slice_in_dim(array, member * BLOCK, BLOCK, 0)
    outgoing = prompt_grads(
        parts,
        block(act),
        base_mine,
        block(cot),
        gain,
        factor_cols[None, :],
        block(scale),
        group_size,
        pieces,
    )
    back = lax.all_to_all(outgoing, dp, 0, 0, tiled=False).astype(F32)
    reduced = jnp.sum(back[:, :, :own_cols], axis=0)
    low_picker = picker.astype(BF16)
    col_all = jnp.concatenate(
        [back[:, pieces : 2 * pieces, half:], back[:, :pieces, half:]], axis=2
    ).reshape(group_size, col_width)
    col_grad = dot(low_picker, col_all.astype(BF16), 0, 0)
    row_part = dot(back[:, 2 * pieces, half : half + BLOCK].astype(BF16), low_picker, 0, 0)
    both = lax.all_gather(jnp.concatenate([reduced, row_part], axis=1), mp, axis=0, tiled=True)
    both = both[:PROMPT].T
    prompt_grad = both[:own_cols].T
    row_grad = both[own_cols:]
    return (
        *adam_step(prompt_master, prompt_first, prompt_second, prompt_grad),
        *adam_step(row_factor, row_first, row_second, row_grad),
        *adam_step(col_factor, col_first, col_second, col_grad),
    )


def solution(mesh):
    ring = 4 if mesh.shape["dp"] % 4 == 0 else 2
    devices = mesh.devices.reshape(mesh.shape["dp"] // ring, ring, mesh.shape["mp"] // 2, 2)
    dp, mp = ROWS_AXES, HEADS_AXES
    return jax.shard_map(
        local,
        mesh=Mesh(devices, dp + mp),
        in_specs=(
            P(dp, None, None),
            P(),
            P(dp, mp),
            P(dp, mp),
            P(dp, mp),
            P(dp, None, mp),
            P(dp, None, None),
            P(None, dp),
            P(None, dp),
            P(None, dp),
            P(dp, None),
            P(dp, None),
            P(dp, None),
            P(dp, mp),
            P(dp, mp),
            P(dp, mp),
            P(dp),
            P(),
        ),
        out_specs=(
            P(None, dp),
            P(None, dp),
            P(None, dp),
            P(dp, None),
            P(dp, None),
            P(dp, None),
            P(dp, mp),
            P(dp, mp),
            P(dp, mp),
        ),
        check_vma=False,
    )
```

time: 1530 us -> 239 us (0.16)
  blocking collectives: 730 us -> 44.2 us
  waiting for transfers between devices: 707 us -> 67.9 us
  starting transfers between devices: 0.46 us -> 54.8 us
  matrix products: 33.7 us -> 11.8 us
    unnamed x7 -> x1, waiting for transfers between devices: 386 us -> 0.02 us
    unnamed x2 -> x0, blocking collectives: 255 us -> none
    all_gather x3 -> x1, waiting for transfers between devices: 244 us -> 3.17 us  [local(): weights_all = lax.all_gather(weights_y, 'z', axis=0, tiled=True)]
    psum x1 -> x0, blocking collectives: 221 us -> none  [local(): row_all, col_all = lax.psum((row_term, col_term), 'dp')]
    all_gather x3, blocking collectives: 254 us -> 44.2 us  [the longest x1 17 us: local(): lax.all_gather(jnp.concatenate([reduced, row_part], axis=1), mp, axis=0,...]
    psum x2 -> x0, waiting for transfers between devices: 77.3 us -> none  [the longest x1 77.3 us: local(): head_total = lax.psum(head_part, 'mp')]
    all_to_all x0 -> x5, waiting for transfers between devices: none -> 64.7 us  [the longest x1 18.5 us: local(): back = lax.all_to_all(outgoing, dp, 0, 0, tiled=False).astype(F32)]
    all_to_all x0 -> x5, starting transfers between devices: none -> 54.8 us  [the longest x1 17.7 us: local(): lax.all_to_all(jnp.broadcast_to(sent[None], (group_size, BLOCK, LANES)),...]
  transfers between devices with their start and end apart: 6 -> 6, of which waited for: 4 -> 5; matrix products, arithmetic and copies ran while one was open for 2% -> 9% of each run, Pallas kernels for 0% -> 0%
where the time goes in v1:
time: 239 us; the launch traced here: 238 us
  waiting for transfers between devices  67.9 us (28%)
  starting transfers between devices  54.8 us (23%)
  blocking collectives  44.2 us (18%)
  between operations  17.7 us (7%)
  other arithmetic  15.7 us (7%)
  local copies, waits for them, and re-layouts  13.3 us (6%)
  Pallas kernels  12.3 us (5%)
  matrix products  11.8 us (5%)
    all_to_all x1, waiting for transfers between devices, local(): back = lax.all_to_all(outgoing, dp, 0, 0, tiled=False).astype(F32)  18.5 us
    all_to_all x1, starting transfers between devices, local(): lax.all_to_all(jnp.broadcast_to(sent[None], (group_size, BLOCK, LANES)),...  17.7 us
    all_gather x1, blocking collectives, local(): lax.all_gather(jnp.concatenate([reduced, row_part], axis=1), mp, axis=0,...  17 us
    all_to_all x1, waiting for transfers between devices, local(): lax.all_to_all(jnp.broadcast_to(sent[None], (group_size, BLOCK, LANES)),...  16.4 us
    all_gather x1, blocking collectives, local(): factor_cols = lax.all_gather(my_cols, mp, axis=0, tiled=True)  15.5 us
    all_to_all x1, waiting for transfers between devices, local(): terms = jnp.sum(lax.all_to_all(terms, dp, 0, 0, tiled=False), axis=0)  15.4 us
    all_to_all x1, waiting for transfers between devices, local(): lax.all_to_all(parts.reshape(groups, BLOCK, width + LANES), mp, 0, 0, til...  14.4 us
    all_to_all x1, starting transfers between devices, local(): lax.all_to_all(jnp.broadcast_to(base_mine[None], (groups, BLOCK, width)),...  13 us
  transfers between devices with their start and end apart: 6, of which 5 were waited for; matrix products, arithmetic and copies ran while one was open for 9% of the time, Pallas kernels for 0%

profile of v1, /device:TPU:1, one launch (start us, length us, event | category | flops | bytes accessed | tf_op | source)
XLA Modules:
  0.0 237.7 jit_solution(16063463930173813452)
XLA Ops:
  8.0 1.3 dynamic_slice.17
  13.6 11.7 %all_gather.12 = bf16[256,768]{1,0:T(8,128)(2,1)} all-gather(bf16[64,768]{1,0:T(8,128)(2,1)S(1)} %pad_maximum_fusion), channel_id=1, replica_groups=mesh['z'=16,'y'=4,'x'=4,'c'=2] {'y'}, dimensions={0}, use_global_device_ids=true | all-gather | bytes 491520 | tf_op jit(solution)/shard_map/all_gather | solution.py:215
  26.2 17.7 %all-to-all-start = ((bf16[64,16,128]{2,1,0:T(8,128)(2,1)}), bf16[64,16,128]{2,1,0:T(8,128)(2,1)S(1)}, u32[]{:S(2)}, u32[]{:S(2)}) async-start(bf16[64,16,128]{2,1,0:T(8,128)(2,1)} %broadcast_in_dim.16), calls=%async_computation | async-start | bytes 524288 | tf_op jit(solution)/shard_map/all_to_all | solution.py:225
  45.0 16.4 %all-to-all-done = bf16[64,16,128]{2,1,0:T(8,128)(2,1)S(1)} async-done(((bf16[64,16,128]{2,1,0:T(8,128)(2,1)}), bf16[64,16,128]{2,1,0:T(8,128)(2,1)S(1)}, u32[]{:S(2)}, u32[]{:S(2)}) %all-to-all-start) | async-done | bytes 262176 | tf_op jit(solution)/shard_map/all_to_all | solution.py:225
  61.4 1.3 fusion.23
  62.7 1.3 compare_reduce_fusion
  67.1 6.3 %all-to-all-start.2 = ((f32[64,8,128]{2,1,0:T(8,128)}), f32[64,8,128]{2,1,0:T(8,128)S(1)}, u32[]{:S(2)}, u32[]{:S(2)}) async-start(f32[64,8,128]{2,1,0:T(8,128)} %maximum_maximum_fusion), calls=%async_computation.2 | async-start | bytes 524288 | tf_op jit(solution)/shard_map/all_to_all | solution.py:249
  75.1 2.6 %fusion = f32[384]{0:T(512)S(1)} fusion(bf16[1,384,4096]{2,1,0:T(8,128)(2,1)} %param.18), kind=kLoop, calls=%fused_computation.2 | loop fusion | flops 4718208 | bytes 3147264 | tf_op jit(solution)/shard_map/reduce_sum | solution.py:256
  78.1 15.4 %all-to-all-done.2 = f32[64,8,128]{2,1,0:T(8,128)S(1)} async-done(((f32[64,8,128]{2,1,0:T(8,128)}), f32[64,8,128]{2,1,0:T(8,128)S(1)}, u32[]{:S(2)}, u32[]{:S(2)}) %all-to-all-start.2) | async-done | bytes 262176 | tf_op jit(solution)/shard_map/all_to_all | solution.py:249
  94.6 13.0 %all-to-all-start.1 = ((bf16[8,16,4096]{2,1,0:T(8,128)(2,1)}), bf16[8,16,4096]{2,1,0:T(8,128)(2,1)S(1)}, u32[]{:S(2)}, u32[]{:S(2)}) async-start(bf16[8,16,4096]{2,1,0:T(8,128)(2,1)} %broadcast_in_dim.18), calls=%async_computation.1 | async-start | bytes 2097152 | tf_op jit(solution)/shard_map/all_to_all | solution.py:229
  107.6 4.7 %fusion.2 = bf16[384,4096]{1,0:T(8,128)(2,1)} fusion(bf16[1,384,4096]{2,1,0:T(8,128)(2,1)} %param.18, f32[4096]{0:T(1024)S(1)} %copy-done.2, f32[384]{0:T(512)S(1)} %add_rsqrt_fusion.1), kind=kLoop, calls=%fused_computation.4 | loop fusion | flops 6291456 | bytes 6309376 | tf_op jit(solution)/shard_map/convert_element_type | solution.py:257
  112.4 15.5 %all-gather = f32[8,1,512]{2,1,0:T(1,128)S(1)} all-gather(f32[1,1,512]{2,1,0:T(1,128)S(1)} %bitcast.66), channel_id=1, replica_groups=mesh['z'=16,'y'=4,'x'=4,'c'=2] {'x','c'}, dimensions={0}, use_global_device_ids=true | all-gather | bytes 18432 | tf_op jit(solution)/shard_map/all_gather | solution.py:252
  128.9 1.5 multiply_convert_fusion
  130.3 3.2 %all-gather.3.cloned.1.call-done.refs_1_ = bf16[4096,768]{1,0:T(8,128)(2,1)} async-done(((bf16[256,768]{1,0:T(8,128)(2,1)}), bf16[4096,768]{1,0:T(8,128)(2,1)}) %all-gather.3.cloned.1.call-update) | async-done | bytes 6291472 | tf_op jit(solution)/shard_map/all_gather | solution.py:224
  133.5 7.5 %fusion.7.qkv_ref = bf16[512,768]{1,0:T(8,128)(2,1)S(1)} fusion(bf16[4096,768]{1,0:T(8,128)(2,1)} %all-gather.3.cloned.1.call-done.refs_1_, bf16[384,4096]{1,0:T(8,128)(2,1)} %fusion.2, bf16[128,4096]{1,0:T(8,128)(2,1)} %get-tuple-element.71), kind=kOutput, calls=%fused_computation.13 | convolution fusion | flops 3230007296 | bytes 11272192 | tf_op jit(solution)/shard_map/dot_general | solution.py:263
  141.0 4.1 %shard_map.241 = (bf16[128,768]{1,0:T(8,128)(2,1)S(1)}, f32[128,128]{1,0:T(8,128)S(1)}) custom-call(bf16[512,768]{1,0:T(8,128)(2,1)S(1)} %fusion.7.qkv_ref, bf16[512,256]{1,0:T(8,128)(2,1)S(1)} %copy-done.1), custom_call_target="tpu_custom_call" | custom-call | tf_op jit(solution)/shard_map/pallas_call | solution.py:72
  145.1 7.1 %shard_map.242 = bf16[128,4224]{1,0:T(8,128)(2,1)S(1)} custom-call(bf16[128,768]{1,0:T(8,128)(2,1)S(1)} %get-tuple-element.15.refs_0_, bf16[4096,768]{1,0:T(8,128)(2,1)} %all-gather.3.cloned.1.call-done.refs_1_, f32[128,128]{1,0:T(8,128)S(1)} %get-tuple-element.16.refs_2_, bf16[128,4096]{1,0:T(8,128)(2,1)S(1)} %get-tuple-element.72.refs_3_, ...), custom_call_target="tpu_custom_call" | custom-call | tf_op jit(solution)/shard_map/pallas_call | solution.py:115
  153.2 7.4 %all-to-all-start.3 = ((bf16[8,16,4224]{2,1,0:T(8,128)(2,1)}), bf16[8,16,4224]{2,1,0:T(8,128)(2,1)S(1)}, u32[]{:S(2)}, u32[]{:S(2)}) async-start(bf16[8,16,4224]{2,1,0:T(8,128)(2,1)} %bitcast.56), calls=%async_computation.3 | async-start | bytes 2162688 | tf_op jit(solution)/shard_map/all_to_all | solution.py:279
  161.6 14.4 %all-to-all-done.3.refs_0_ = bf16[8,16,4224]{2,1,0:T(8,128)(2,1)S(1)} async-done(((bf16[8,16,4224]{2,1,0:T(8,128)(2,1)}), bf16[8,16,4224]{2,1,0:T(8,128)(2,1)S(1)}, u32[]{:S(2)}, u32[]{:S(2)}) %all-to-all-start.3) | async-done | bytes 1081376 | tf_op jit(solution)/shard_map/all_to_all | solution.py:279
  176.0 1.2 shard_map.243
  177.2 10.4 %all-to-all-start.4 = ((bf16[64,16,128]{2,1,0:T(8,128)(2,1)}), bf16[64,16,128]{2,1,0:T(8,128)(2,1)S(1)}, u32[]{:S(2)}, u32[]{:S(2)}) async-start(bf16[64,16,128]{2,1,0:T(8,128)(2,1)} %shard_map.243), calls=%async_computation.4 | async-start | bytes 524288 | tf_op jit(solution)/shard_map/all_to_all | solution.py:294
  188.3 18.5 %all-to-all-done.4 = bf16[64,16,128]{2,1,0:T(8,128)(2,1)S(1)} async-done(((bf16[64,16,128]{2,1,0:T(8,128)(2,1)}), bf16[64,16,128]{2,1,0:T(8,128)(2,1)S(1)}, u32[]{:S(2)}, u32[]{:S(2)}) %all-to-all-start.4) | async-done | bytes 262176 | tf_op jit(solution)/shard_map/all_to_all | solution.py:294
  207.3 17.0 %all_gather.15 = f32[128,128]{1,0:T(8,128)S(1)} all-gather(f32[16,128]{1,0:T(8,128)S(1)} %pad_maximum_fusion.2), channel_id=1, replica_groups=mesh['z'=16,'y'=4,'x'=4,'c'=2] {'x','c'}, dimensions={0}, use_global_device_ids=true | all-gather | bytes 73728 | tf_op jit(solution)/shard_map/all_gather | solution.py:302
  228.9 2.0 divide_subtract_fusion
  (89 shorter events, 18.7 us)
Async XLA Ops:
  7.2 67.1 %copy-start.3 = (bf16[1,100,4096]{2,1,0:T(8,128)(2,1)S(1)}, bf16[1,100,4096]{2,1,0:T(8,128)(2,1)}, u32[]{:S(2)}) copy-start(bf16[1,100,4096]{2,1,0:T(8,128)(2,1)} %param.24) | copy-start | bytes 2457604
  7.2 126.3 %all-gather.3.cloned.1.call-start = ((), (), s32[]{:S(2)}) async-start(), calls=%async_computation.5 | async-start | bytes 6684672 | tf_op jit(solution)/shard_map/all_gather | solution.py:224
  26.2 35.2 %all-to-all-start = ((bf16[64,16,128]{2,1,0:T(8,128)(2,1)}), bf16[64,16,128]{2,1,0:T(8,128)(2,1)S(1)}, u32[]{:S(2)}, u32[]{:S(2)}) async-start(bf16[64,16,128]{2,1,0:T(8,128)(2,1)} %broadcast_in_dim.16), calls=%async_computation | async-start | bytes 524288 | tf_op jit(solution)/shard_map/all_to_all | solution.py:225
  67.1 26.4 %all-to-all-start.2 = ((f32[64,8,128]{2,1,0:T(8,128)}), f32[64,8,128]{2,1,0:T(8,128)S(1)}, u32[]{:S(2)}, u32[]{:S(2)}) async-start(f32[64,8,128]{2,1,0:T(8,128)} %maximum_maximum_fusion), calls=%async_computation.2 | async-start | bytes 524288 | tf_op jit(solution)/shard_map/all_to_all | solution.py:249
  77.7 29.9 %copy-start.2 = (f32[4096]{0:T(1024)S(1)}, f32[4096]{0:T(1024)}, u32[]{:S(2)}) copy-start(f32[4096]{0:T(1024)} %param.19) | copy-start | bytes 49156
  94.6 33.4 %all-to-all-start.1 = ((bf16[8,16,4096]{2,1,0:T(8,128)(2,1)}), bf16[8,16,4096]{2,1,0:T(8,128)(2,1)S(1)}, u32[]{:S(2)}, u32[]{:S(2)}) async-start(bf16[8,16,4096]{2,1,0:T(8,128)(2,1)} %broadcast_in_dim.18), calls=%async_computation.1 | async-start | bytes 2097152 | tf_op jit(solution)/shard_map/all_to_all | solution.py:229
  133.5 7.5 %copy-start.1 = (bf16[512,256]{1,0:T(8,128)(2,1)S(1)}, bf16[512,256]{1,0:T(8,128)(2,1)}, u32[]{:S(2)}) copy-start(bf16[512,256]{1,0:T(8,128)(2,1)} %fusion.11.up_ref) | copy-start | bytes 786436
  152.2 1.0 copy-start
  153.2 34.5 %copy-start.5 = (f32[100,64]{0,1:T(8,128)S(1)}, f32[100,64]{0,1:T(8,128)}, u32[]{:S(2)}) copy-start(f32[100,64]{0,1:T(8,128)} %param.25) | copy-start | bytes 76804
  153.2 34.6 %copy-start.6 = (f32[64,100]{1,0:T(8,128)S(1)}, f32[64,100]{1,0:T(8,128)}, u32[]{:S(2)}) copy-start(f32[64,100]{1,0:T(8,128)} %param.28) | copy-start | bytes 76804
  153.2 34.7 %copy-start.7 = (f32[100,64]{0,1:T(8,128)S(1)}, f32[100,64]{0,1:T(8,128)}, u32[]{:S(2)}) copy-start(f32[100,64]{0,1:T(8,128)} %param.26) | copy-start | bytes 76804
  153.2 34.8 %copy-start.8 = (f32[100,64]{0,1:T(8,128)S(1)}, f32[100,64]{0,1:T(8,128)}, u32[]{:S(2)}) copy-start(f32[100,64]{0,1:T(8,128)} %param.27) | copy-start | bytes 76804
  153.2 34.9 %copy-start.9 = (f32[64,100]{1,0:T(8,128)S(1)}, f32[64,100]{1,0:T(8,128)}, u32[]{:S(2)}) copy-start(f32[64,100]{1,0:T(8,128)} %param.29) | copy-start | bytes 76804
  153.2 35.0 %copy-start.10 = (f32[64,100]{1,0:T(8,128)S(1)}, f32[64,100]{1,0:T(8,128)}, u32[]{:S(2)}) copy-start(f32[64,100]{1,0:T(8,128)} %param.30) | copy-start | bytes 76804
  153.2 22.8 %all-to-all-start.3 = ((bf16[8,16,4224]{2,1,0:T(8,128)(2,1)}), bf16[8,16,4224]{2,1,0:T(8,128)(2,1)S(1)}, u32[]{:S(2)}, u32[]{:S(2)}) async-start(bf16[8,16,4224]{2,1,0:T(8,128)(2,1)} %bitcast.56), calls=%async_computation.3 | async-start | bytes 2162688 | tf_op jit(solution)/shard_map/all_to_all | solution.py:279
  160.6 68.3 %copy-start.4 = (f32[64,512]{1,0:T(8,128)S(1)}, f32[64,512]{1,0:T(8,128)}, u32[]{:S(2)}) copy-start(f32[64,512]{1,0:T(8,128)} %param.31) | copy-start | bytes 393220
  160.6 68.3 %copy-start.11 = (f32[64,512]{1,0:T(8,128)S(1)}, f32[64,512]{1,0:T(8,128)}, u32[]{:S(2)}) copy-start(f32[64,512]{1,0:T(8,128)} %param.32) | copy-start | bytes 393220
  177.2 29.5 %all-to-all-start.4 = ((bf16[64,16,128]{2,1,0:T(8,128)(2,1)}), bf16[64,16,128]{2,1,0:T(8,128)(2,1)S(1)}, u32[]{:S(2)}, u32[]{:S(2)}) async-start(bf16[64,16,128]{2,1,0:T(8,128)(2,1)} %shard_map.243), calls=%async_computation.4 | async-start | bytes 524288 | tf_op jit(solution)/shard_map/all_to_all | solution.py:294
Sparse Core Ops, SparseCore 0:
  25.6 107.8 all-gather.2

commit v2 on v1

v2 whole, which is shorter than its diff:
```python
import jax
import jax.numpy as jnp
from jax import lax
from jax.experimental import pallas as pl
from jax.experimental.pallas import tpu as pltpu
from jax.sharding import Mesh, PartitionSpec as P

HEAD_DIM = 64
PROMPT = 100
PAD = 128
BLOCK = 16
LANES = 128
HALF = 64
CHUNKS = 4

beta_first = 0.9
beta_second = 0.99
learn_rate = 0.01
adam_epsilon = 1e-08
norm_epsilon = 1e-06

ROWS_AXES = ("z", "y")
HEADS_AXES = ("x", "c")
BF16 = jnp.bfloat16
F32 = jnp.float32
VMEM = pl.BlockSpec(memory_space=pltpu.VMEM)
SMEM = pl.BlockSpec(memory_space=pltpu.SMEM)
PARAMS = pltpu.CompilerParams(vmem_limit_bytes=50 * 1024 * 1024)


def adam_step(param, moment_one, moment_two, gradient):
    first_new = beta_first * moment_one + (1.0 - beta_first) * gradient
    second_new = beta_second * moment_two + (1.0 - beta_second) * gradient * gradient
    return (
        param - learn_rate * first_new / (jnp.sqrt(second_new) + adam_epsilon),
        first_new,
        second_new,
    )


def dot(a, b, da, db, precision=None):
    return lax.dot_general(
        a, b, (((da,), (db,)), ((), ())), preferred_element_type=F32, precision=precision
    )


def iota(shape, axis):
    return lax.broadcasted_iota(jnp.int32, shape, axis)


def swap_halves(array):
    return jnp.concatenate([array[:, HALF:], array[:, :HALF]], axis=1)


def as_column(line):
    size = line.shape[1]
    eye = iota((size, size), 0) == iota((size, size), 1)
    return jnp.sum(jnp.where(eye, line, 0.0), axis=1, keepdims=True)


def factor_kernel(first_ref, slot_ref, row_ref, col_ref, out_ref):
    owned, width = col_ref.shape
    count = slot_ref.shape[1]
    pieces = width // LANES
    picker = (slot_ref[...] - first_ref[0] == iota((owned, count), 0)).astype(F32)
    high = lax.Precision.HIGHEST
    cols = dot(picker, col_ref[...], 0, 0, high)
    rows = dot(picker, row_ref[...], 0, 0, high)
    rows = jnp.concatenate([rows, jnp.zeros((count, LANES - PROMPT), F32)], axis=1)
    for piece in range(pieces):
        out_ref[:, piece, :] = cols[:, piece * LANES : (piece + 1) * LANES]
    out_ref[:, pieces, :] = rows
    for piece in range(pieces + 1, out_ref.shape[1]):
        out_ref[:, piece, :] = jnp.zeros((count, LANES), F32)


def main_kernel(
    place_ref,
    weight_hbm,
    hidden_ref,
    up_ref,
    cols_ref,
    rows_ref,
    gain_ref,
    cot_ref,
    keep_ref,
    send_ref,
    unit_out,
    base_out,
    scale_out,
    line_out,
    weights,
    base,
    unit,
    normed,
    total,
    qkv,
    parts,
    scale,
    sems,
):
    width = hidden_ref.shape[1]
    tokens = hidden_ref.shape[0]
    length = PAD + tokens
    inner = up_ref.shape[1]
    three = 3 * inner
    depth = width // CHUNKS
    groups = cols_ref.shape[0]
    size = width // groups
    pieces = size // LANES
    member = place_ref[0]
    core = place_ref[1]

    copies = [
        pltpu.make_async_copy(
            weight_hbm.at[pl.ds(k * depth, depth), :],
            weights.at[pl.ds(k * depth, depth), :],
            sems.at[k],
        )
        for k in range(CHUNKS)
    ]
    for copy in copies:
        copy.start()
    line = jnp.concatenate(
        [cols_ref[g, k : k + 1, :] for g in range(groups) for k in range(pieces)], axis=1
    )
    line_out[...] = line
    rows = as_column(rows_ref[...])
    own = pl.ds(pl.multiple_of(member * BLOCK, BLOCK), BLOCK)
    squares = jnp.zeros((PAD, 1), F32)
    for k in range(CHUNKS):
        copies[k].wait()
        span = slice(k * depth, (k + 1) * depth)
        part = dot(hidden_ref[:, span], weights[span, :three], 1, 0)
        if k == 0:
            total[...] = part
        elif k < CHUNKS - 1:
            total[...] += part
        else:
            qkv[PAD:, :] = (total[...] + part).astype(BF16)
        base_part = jnp.transpose(weights[span, three:].astype(F32))
        base[:, span] = base_part
        act = (base_part * rows * line[:, span]).astype(BF16).astype(F32)
        unit[:, span] = act
        squares = squares + jnp.sum(act * act, axis=1, keepdims=True)
    inverse = lax.rsqrt(squares * (1.0 / width) + norm_epsilon)
    scale[...] = jnp.where(iota((PAD, LANES), 1) == 0, inverse, rows)
    scale_own = scale[own, :]
    scale_out[...] = scale_own
    for k in range(CHUNKS):
        span = slice(k * depth, (k + 1) * depth)
        unit_part = unit[:, span] * inverse
        unit[:, span] = unit_part
        normed[:, span] = (unit_part * gain_ref[:, span]).astype(BF16)
    qkv[:PAD, :] = dot(normed[...], weights[:, :three], 1, 0).astype(BF16)

    column = iota((length, length), 1)
    real_key = (column < PROMPT) | (column >= PAD)
    along = jnp.zeros((PAD, 1), F32)
    grads = [[], [], []]
    for head in range(inner // HEAD_DIM):
        at = head * HEAD_DIM
        query = qkv[:, at : at + HEAD_DIM]
        key = qkv[:, inner + at : inner + at + HEAD_DIM]
        value = qkv[:, 2 * inner + at : 2 * inner + at + HEAD_DIM]
        up = up_ref[:, at : at + HEAD_DIM]
        exponent = jnp.where(real_key, jnp.exp(dot(query, key, 1, 1)), 0.0)
        attend = exponent / jnp.sum(exponent, axis=1, keepdims=True)
        grad_prob = dot(up, value, 1, 1)
        row_dot = jnp.sum(attend * grad_prob, axis=1, keepdims=True)
        grad_score = (attend * (grad_prob - row_dot)).astype(BF16)
        found = (
            dot(grad_score[:PAD, :], key, 1, 0).astype(BF16),
            dot(grad_score[:, :PAD], query, 0, 0).astype(BF16),
            dot(attend[:, :PAD].astype(BF16), up, 0, 0).astype(BF16),
        )
        for kind, (grad, low) in enumerate(zip(found, (query, key, value))):
            grads[kind].append(grad)
            along = along + jnp.sum(
                grad.astype(F32) * low[:PAD].astype(F32), axis=1, keepdims=True
            )
    grad_all = jnp.concatenate(grads[0] + grads[1] + grads[2], axis=1)

    mean = along * (1.0 / width)
    strength = inverse * rows
    for g in range(groups):
        span = slice(g * size, (g + 1) * size)
        part = dot(grad_all, weights[span, :three], 1, 1)
        parts[:, span] = part
        weighted = base[:, span] * strength
        base_own = base[own, span]
        base_out[:, span] = base_own
        unit_out[:, span] = unit[own, span]
        cols = (
            gain_ref[:, span] * jnp.sum(part * weighted, axis=0, keepdims=True)
            - jnp.sum(weighted * unit[:, span] * mean, axis=0, keepdims=True)
            + jnp.sum(
                cot_ref[:, span].astype(F32) * base_own * scale_own[:, 1:2], axis=0, keepdims=True
            )
        )
        parts[g * BLOCK : (g + 1) * BLOCK, width:] = jnp.concatenate(
            [cols[:, at : at + LANES] for at in range(0, size, LANES)]
            + [jnp.zeros((BLOCK - pieces, LANES), F32)],
            axis=0,
        )
    for pair in range(groups // 2):
        start = pl.multiple_of((2 * pair + core) * BLOCK, BLOCK)
        keep_ref[pair, :, :] = parts[pl.ds(start, BLOCK), :]
        start = pl.multiple_of((2 * pair + 1 - core) * BLOCK, BLOCK)
        send_ref[pair, :, :] = parts[pl.ds(start, BLOCK), :]


def main_part(place, weights, hidden, up, cols, rows, gain, cot):
    width = hidden.shape[1]
    length = PAD + hidden.shape[0]
    three = 3 * up.shape[1]
    groups = cols.shape[0]
    half = jax.ShapeDtypeStruct((groups // 2, BLOCK, width + LANES), F32)
    own = jax.ShapeDtypeStruct((BLOCK, width), F32)
    return pl.pallas_call(
        main_kernel,
        out_shape=(
            half,
            half,
            own,
            own,
            jax.ShapeDtypeStruct((BLOCK, LANES), F32),
            jax.ShapeDtypeStruct((1, width), F32),
        ),
        in_specs=[SMEM, pl.BlockSpec(memory_space=pl.ANY)] + [VMEM] * 6,
        out_specs=(VMEM,) * 6,
        scratch_shapes=[
            pltpu.VMEM(weights.shape, BF16),
            pltpu.VMEM((PAD, width), F32),
            pltpu.VMEM((PAD, width), F32),
            pltpu.VMEM((PAD, width), BF16),
            pltpu.VMEM((length - PAD, three), F32),
            pltpu.VMEM((length, three), BF16),
            pltpu.VMEM((PAD, width + LANES), F32),
            pltpu.VMEM((PAD, LANES), F32),
            pltpu.SemaphoreType.DMA((CHUNKS,)),
        ],
        compiler_params=PARAMS,
    )(place, weights, hidden, up, cols, rows, gain, cot)


def prompt_kernel(pieces, got_ref, unit_ref, base_ref, cot_ref, gain_ref, cols_ref, scale_ref, out_ref):
    width = unit_ref.shape[1]
    total = got_ref[0, :, :].astype(F32)
    for source in range(1, got_ref.shape[0]):
        total = total + got_ref[source, :, :].astype(F32)
    inverse = scale_ref[:, 0:1]
    rows = scale_ref[:, 1:2]
    unit = unit_ref[...]
    scaled = total[:, :width] * gain_ref[...]
    mean = jnp.sum(scaled * unit, axis=1, keepdims=True) * (1.0 / width)
    grad = cot_ref[...].astype(F32) + inverse * (scaled - unit * mean)
    times_cols = grad * cols_ref[...]
    grad_rows = jnp.sum(times_cols * base_ref[...], axis=1, keepdims=True)
    grad_base = times_cols * rows
    cols = total[:pieces, width:]
    spare = BLOCK - 2 * pieces
    line = jnp.sum(
        jnp.where(iota((BLOCK, LANES), 1) == iota((BLOCK, LANES), 0) + HALF, grad_rows, 0.0),
        axis=0,
        keepdims=True,
    )
    under = jnp.where(iota((spare, LANES), 0) == 0, line, 0.0)
    tail = jnp.concatenate([cols, swap_halves(cols), under], axis=0)
    first_half = iota((BLOCK, LANES), 1) < HALF
    for pair in range(width // LANES):
        block = grad_base[:, pair * LANES : (pair + 1) * LANES]
        out_ref[2 * pair, :, :] = jnp.where(first_half, block, tail).astype(BF16)
        out_ref[2 * pair + 1, :, :] = jnp.where(first_half, swap_halves(block), tail).astype(BF16)


def owner_kernel(first_ref, slot_ref, back_ref, shared_ref, col_ref):
    owned, width = col_ref.shape
    count = slot_ref.shape[1]
    pieces = width // LANES
    picker = (slot_ref[...] - first_ref[0] == iota((owned, count), 0)).astype(BF16)
    back = back_ref[...].astype(F32)
    total = jnp.sum(back, axis=0)
    first_half = iota((owned, LANES), 1) < HALF
    for piece in range(pieces):
        upper = dot(picker, back[:, piece, :].astype(BF16), 1, 0)
        lower = dot(picker, back[:, pieces + piece, :].astype(BF16), 1, 0)
        col_ref[:, piece * LANES : (piece + 1) * LANES] = jnp.where(
            first_half, swap_halves(lower), upper
        )
    rows = dot(back[:, 2 * pieces, :].astype(BF16), picker, 0, 1)
    shared_ref[...] = jnp.concatenate([total[:, :HALF], rows[HALF : HALF + BLOCK, :]], axis=1)


def update_kernel(grads_ref, *refs):
    grads = jnp.transpose(grads_ref[...])
    for kind in range(2):
        param, one, two, param_out, one_out, two_out = refs[kind::2]
        rows = param.shape[0]
        found = grads[kind * HALF : kind * HALF + rows, : param.shape[1]]
        param_out[...], one_out[...], two_out[...] = adam_step(param[...], one[...], two[...], found)


def local(
    hidden_rows,
    norm_gain,
    w_query,
    w_key,
    w_value,
    head_cotangent,
    prompt_cotangent,
    prompt_master,
    prompt_first,
    prompt_second,
    row_factor,
    row_first,
    row_second,
    col_factor,
    col_first,
    col_second,
    row_tenant,
    tenant_slot,
):
    dp, mp = ROWS_AXES, HEADS_AXES
    count = lax.axis_size(dp)
    groups = lax.axis_size(mp)
    device = lax.axis_index(dp)
    member = lax.axis_index(mp)
    owned, col_width = col_factor.shape
    width = hidden_rows.shape[2]
    pieces = col_width // LANES
    padding = ((0, 0), (0, LANES - PROMPT))

    weights = jnp.concatenate(
        [w_query, w_key, w_value, jnp.pad(prompt_master.T.astype(BF16), padding)], axis=1
    )
    weights = lax.all_gather(weights, "y", axis=0, tiled=True)
    slot = lax.dynamic_index_in_dim(tenant_slot, row_tenant[0], 0, keepdims=False)
    weights, slot = lax.optimization_barrier((weights, slot))
    weights = lax.all_gather(weights, "z", axis=0, tiled=True)

    slots = lax.psum(jnp.where(lax.iota(jnp.int32, count) == device, slot, 0), dp)[None, :]
    first = (device * owned).astype(jnp.int32).reshape(1)
    terms = pl.pallas_call(
        factor_kernel,
        out_shape=jax.ShapeDtypeStruct((count, 8, LANES), F32),
        in_specs=[SMEM, VMEM, VMEM, VMEM],
        out_specs=VMEM,
        compiler_params=PARAMS,
    )(first, slots, row_factor, col_factor)
    terms = jnp.sum(lax.all_to_all(terms, dp, 0, 0, tiled=False), axis=0)
    factor_cols = lax.all_to_all(
        jnp.broadcast_to(terms[None], (groups, 8, LANES)), mp, 0, 0, tiled=False
    )
    factor_rows = terms[pieces : pieces + 1]

    gain = norm_gain[None, :]
    hidden = hidden_rows[0].astype(F32)
    inverse = lax.rsqrt(jnp.mean(hidden * hidden, axis=-1, keepdims=True) + norm_epsilon)
    hidden = (hidden * inverse * gain).astype(BF16)
    upstream = jnp.concatenate(
        [
            jnp.pad(head_cotangent[0, :PROMPT], ((0, PAD - PROMPT), (0, 0))),
            head_cotangent[0, PROMPT:],
        ],
        axis=0,
    )
    cot = lax.dynamic_slice_in_dim(
        jnp.pad(prompt_cotangent[0], ((0, PAD - PROMPT), (0, 0))), member * BLOCK, BLOCK, 0
    )
    place = jnp.stack([member, lax.axis_index("c")]).astype(jnp.int32)
    keep, send, unit_own, base_own, scale_own, line = main_part(
        place, weights, hidden, upstream, factor_cols, factor_rows, gain, cot
    )

    parts = (keep + lax.ppermute(send, "c", [(0, 1), (1, 0)])).astype(BF16)
    parts = lax.all_to_all(parts, "x", 0, 0, tiled=False)
    outgoing = pl.pallas_call(
        lambda *refs: prompt_kernel(pieces, *refs),
        out_shape=jax.ShapeDtypeStruct((count, BLOCK, LANES), BF16),
        in_specs=[VMEM] * 7,
        out_specs=VMEM,
        compiler_params=PARAMS,
    )(parts, unit_own, base_own, cot, gain, line, scale_own)

    back = lax.all_to_all(outgoing, dp, 0, 0, tiled=False)
    shared, col_grad = pl.pallas_call(
        owner_kernel,
        out_shape=(
            jax.ShapeDtypeStruct((BLOCK, LANES), F32),
            jax.ShapeDtypeStruct((owned, col_width), F32),
        ),
        in_specs=[SMEM, VMEM, VMEM],
        out_specs=(VMEM, VMEM),
        compiler_params=PARAMS,
    )(first, slots, back)
    shared = lax.all_to_all(
        jnp.broadcast_to(shared[None], (groups, BLOCK, LANES)), mp, 0, 0, tiled=False
    ).reshape(PAD, LANES)
    operands = [
        part
        for pair in zip(
            (prompt_master.T, prompt_first.T, prompt_second.T), (row_factor, row_first, row_second)
        )
        for part in pair
    ]
    new = pl.pallas_call(
        update_kernel,
        out_shape=tuple(jax.ShapeDtypeStruct(part.shape, F32) for part in operands),
        in_specs=[VMEM] * 7,
        out_specs=(VMEM,) * 6,
        compiler_params=PARAMS,
    )(shared, *operands)
    return (
        *(part.T for part in new[0::2]),
        *new[1::2],
        *adam_step(col_factor, col_first, col_second, col_grad),
    )


def solution(mesh):
    ring = 4 if mesh.shape["dp"] % 4 == 0 else 2
    devices = mesh.devices.reshape(mesh.shape["dp"] // ring, ring, mesh.shape["mp"] // 2, 2)
    dp, mp = ROWS_AXES, HEADS_AXES
    return jax.shard_map(
        local,
        mesh=Mesh(devices, dp + mp),
        in_specs=(
            P(dp, None, None),
            P(),
            P(dp, mp),
            P(dp, mp),
            P(dp, mp),
            P(dp, None, mp),
            P(dp, None, None),
            P(None, dp),
            P(None, dp),
            P(None, dp),
            P(dp, None),
            P(dp, None),
            P(dp, None),
            P(dp, mp),
            P(dp, mp),
            P(dp, mp),
            P(dp),
            P(),
        ),
        out_specs=(
            P(None, dp),
            P(None, dp),
            P(None, dp),
            P(dp, None),
            P(dp, None),
            P(dp, None),
            P(dp, mp),
            P(dp, mp),
            P(dp, mp),
        ),
        check_vma=False,
    )
```

time: 239 us -> 222 us (0.929)
  blocking collectives: 44.2 us -> 82.3 us
  starting transfers between devices: 54.8 us -> 34.9 us
  waiting for transfers between devices: 67.9 us -> 55.8 us
  matrix products: 11.8 us -> 0 us
  local copies, waits for them, and re-layouts: 13.3 us -> 6.1 us
  other arithmetic: 15.7 us -> 10.6 us
  Pallas kernels: 12.3 us -> 16.1 us
  between operations: 17.7 us -> 14.9 us
    all_to_all x0 -> x2, blocking collectives: none -> 42.5 us  [the longest x1 29.9 us: local(): back = lax.all_to_all(outgoing, dp, 0, 0, tiled=False)]
    all_to_all x4 -> x2, waiting for transfers between devices: 49.3 us -> 8.76 us  [the longest x1 4.68 us: local(): lax.all_to_all(jnp.broadcast_to(terms[None], (groups, 8, LANES)), mp, 0,...]
    all_gather x3 -> x1, blocking collectives: 44.2 us -> 12.4 us  [local(): weights = lax.all_gather(weights, 'y', axis=0, tiled=True)]
    all_gather x1, waiting for transfers between devices: 3.17 us -> 34 us  [local(): weights = lax.all_gather(weights, 'z', axis=0, tiled=True)]
    psum x0 -> x1, blocking collectives: none -> 27.4 us  [local(): lax.psum(jnp.where(lax.iota(jnp.int32, count) == device, slot, 0), dp)]
    all_to_all x4 -> x2, starting transfers between devices: 48.5 us -> 23.8 us  [the longest x1 15.1 us: local(): lax.all_to_all(jnp.broadcast_to(terms[None], (groups, 8, LANES)), mp, 0,...]
    dot_general x5 -> x0, matrix products: 11.8 us -> none  [the longest x1 7.5 us: local(): qkv = jnp.dot(normed, weights_all, preferred_element_type=F32).astype(BF16)]
    all_to_all x1, waiting for transfers between devices: 15.4 us -> 10.7 us  [local(): terms = jnp.sum(lax.all_to_all(terms, dp, 0, 0, tiled=False), axis=0)]
  transfers between devices with their start and end apart: 6 -> 5, of which waited for: 5 -> 5; matrix products, arithmetic and copies ran while one was open for 9% -> 5% of each run, Pallas kernels for 0% -> 1%
where the time goes in v2:
time: 222 us; the launch traced here: 221 us
  blocking collectives  82.3 us (37%)
  waiting for transfers between devices  55.8 us (25%)
  starting transfers between devices  34.9 us (16%)
  Pallas kernels  16.1 us (7%)
  between operations  14.9 us (7%)
  other arithmetic  10.6 us (5%)
  local copies, waits for them, and re-layouts  6.1 us (3%)
    all_gather x1, waiting for transfers between devices, local(): weights = lax.all_gather(weights, 'z', axis=0, tiled=True)  34 us
    all_to_all x1, blocking collectives, local(): back = lax.all_to_all(outgoing, dp, 0, 0, tiled=False)  29.9 us
    psum x1, blocking collectives, local(): lax.psum(jnp.where(lax.iota(jnp.int32, count) == device, slot, 0), dp)  27.4 us
    all_to_all x1, starting transfers between devices, local(): lax.all_to_all(jnp.broadcast_to(terms[None], (groups, 8, LANES)), mp, 0,...  15.1 us
    pallas_call x1, Pallas kernels, main_part(): pl.pallas_call(main_kernel, out_shape=(half, half, own, own, jax.ShapeDty...  13.4 us
    all_to_all x1, blocking collectives, local(): parts = lax.all_to_all(parts, 'x', 0, 0, tiled=False)  12.6 us
    all_gather x1, blocking collectives, local(): weights = lax.all_gather(weights, 'y', axis=0, tiled=True)  12.4 us
    all_to_all x1, waiting for transfers between devices, local(): terms = jnp.sum(lax.all_to_all(terms, dp, 0, 0, tiled=False), axis=0)  10.7 us
  transfers between devices with their start and end apart: 5, of which 5 were waited for; matrix products, arithmetic and copies ran while one was open for 5% of the time, Pallas kernels for 1%

profile of v2, /device:TPU:1, one launch (start us, length us, event | category | flops | bytes accessed | tf_op | source)
XLA Modules:
  0.0 220.6 jit_solution(7589874688157323399)
XLA Ops:
  8.6 0.8 fusion.7
  9.4 12.4 %all_gather.6 = bf16[256,896]{1,0:T(8,128)(2,1)} all-gather(bf16[64,896]{1,0:T(8,128)(2,1)S(1)} %fusion.7), channel_id=1, replica_groups=mesh['z'=16,'y'=4,'x'=4,'c'=2] {'y'}, dimensions={0}, use_global_device_ids=true | all-gather | bytes 573440 | tf_op jit(solution)/shard_map/all_gather | solution.py:337
  21.9 1.3 dynamic_slice.7
  23.8 27.4 %psum.7.slot_ref = s32[1,64]{1,0:T(1,128)S(1)} all-reduce(s32[1,64]{1,0:T(1,128)S(1)} %fusion.8), channel_id=1, replica_groups=mesh['z'=16,'y'=4,'x'=4,'c'=2] {'z','y'}, use_global_device_ids=true, to_apply=%region_0.1 | all-reduce | flops 64 | bytes 512 | tf_op jit(solution)/shard_map/psum | solution.py:342
  51.2 0.9 copy-done
  52.9 1.2 shard_map.241
  54.0 8.3 %all-to-all-start = ((f32[64,8,128]{2,1,0:T(8,128)}), f32[64,8,128]{2,1,0:T(8,128)S(1)}, u32[]{:S(2)}, u32[]{:S(2)}) async-start(f32[64,8,128]{2,1,0:T(8,128)} %shard_map.241), calls=%async_computation | async-start | bytes 524288 | tf_op jit(solution)/shard_map/all_to_all | solution.py:351
  62.4 0.8 slice_bitcast_fusion.1
  63.2 1.0 slice_bitcast_fusion
  64.2 2.6 %fusion = f32[384]{0:T(512)S(1)} fusion(bf16[1,384,4096]{2,1,0:T(8,128)(2,1)} %param.18), kind=kLoop, calls=%fused_computation.2 | loop fusion | flops 4718208 | bytes 3147264 | tf_op jit(solution)/shard_map/reduce_sum | solution.py:359
  66.9 4.7 %fusion.2.hidden_ref = bf16[384,4096]{1,0:T(8,128)(2,1)} fusion(bf16[1,384,4096]{2,1,0:T(8,128)(2,1)} %param.18, f32[4096]{0:T(1024)S(1)} %copy-done.2, f32[384]{0:T(512)S(1)} %add_rsqrt_fusion), kind=kLoop, calls=%fused_computation.4 | loop fusion | flops 6291456 | bytes 6309376 | tf_op jit(solution)/shard_map/convert_element_type | solution.py:360
  71.6 10.7 %all-to-all-done = f32[64,8,128]{2,1,0:T(8,128)S(1)} async-done(((f32[64,8,128]{2,1,0:T(8,128)}), f32[64,8,128]{2,1,0:T(8,128)S(1)}, u32[]{:S(2)}, u32[]{:S(2)}) %all-to-all-start) | async-done | bytes 262176 | tf_op jit(solution)/shard_map/all_to_all | solution.py:351
  83.0 15.1 %all-to-all-start.1 = ((f32[8,8,128]{2,1,0:T(8,128)}), f32[8,8,128]{2,1,0:T(8,128)S(1)}, u32[]{:S(2)}, u32[]{:S(2)}) async-start(f32[8,8,128]{2,1,0:T(8,128)} %broadcast_in_dim.30), calls=%async_computation.1 | async-start | bytes 65536 | tf_op jit(solution)/shard_map/all_to_all | solution.py:352
  98.2 4.7 %all-to-all-done.1.cols_ref = f32[8,8,128]{2,1,0:T(8,128)S(1)} async-done(((f32[8,8,128]{2,1,0:T(8,128)}), f32[8,8,128]{2,1,0:T(8,128)S(1)}, u32[]{:S(2)}, u32[]{:S(2)}) %all-to-all-start.1) | async-done | bytes 32800 | tf_op jit(solution)/shard_map/all_to_all | solution.py:352
  102.9 34.0 %all-gather.2.cloned.1.call-done.weight_hbm = bf16[4096,896]{1,0:T(8,128)(2,1)} async-done(((bf16[256,896]{1,0:T(8,128)(2,1)}), bf16[4096,896]{1,0:T(8,128)(2,1)}) %all-gather.2.cloned.1.call-update) | async-done | bytes 7340048 | tf_op jit(solution)/shard_map/all_gather | solution.py:340
  136.9 13.4 %shard_map.242 = (f32[4,16,4224]{2,1,0:T(8,128)S(1)}, f32[4,16,4224]{2,1,0:T(8,128)S(1)}, f32[16,4096]{1,0:T(8,128)S(1)}, f32[16,4096]{1,0:T(8,128)S(1)}, f32[16,128]{1,0:T(8,128)S(1)}, /*index=5*/f32[1,4096]{1,0:T(1,128)S(1)}) custom-call(s32[2]{0:T(128)S(1)} %pad_add_fusion.place_ref, bf16[4096,896]{1,0:T(8,128)(2,1)} %all-gather.2.cloned.1.call-done.weight_hbm, ...), custom_call_target="tpu_custom_call" | custom-call | tf_op jit(solution)/shard_map/pallas_call | solution.py:220
  150.3 2.7 %collective-permute-start = (f32[4,16,4224]{2,1,0:T(8,128)S(1)}, f32[4,16,4224]{2,1,0:T(8,128)S(1)}, u32[]{:S(2)}, u32[]{:S(2)}) collective-permute-start(f32[4,16,4224]{2,1,0:T(8,128)S(1)} %get-tuple-element.28), channel_id=1, source_target_pairs={{0,1},{1,0},{2,3},{3,2},{4,5},{5,4},{6,7},{7,6},{8,9},{9,8},{10,11... | collective-permute-start | bytes 3244040 | tf_op jit(solution)/shard_map/ppermute | solution.py:376
  153.1 2.3 %collective-permute-done = f32[4,16,4224]{2,1,0:T(8,128)S(1)} collective-permute-done((f32[4,16,4224]{2,1,0:T(8,128)S(1)}, f32[4,16,4224]{2,1,0:T(8,128)S(1)}, u32[]{:S(2)}, u32[]{:S(2)}) %collective-permute-start) | collective-permute-done | bytes 1081376 | tf_op jit(solution)/shard_map/ppermute | solution.py:376
  155.5 12.6 %all_to_all.25.refs_0_ = bf16[4,16,4224]{2,1,0:T(8,128)(2,1)S(1)} all-to-all(bf16[4,16,4224]{2,1,0:T(8,128)(2,1)S(1)} %add_convert_fusion), channel_id=1, replica_groups=mesh['z'=16,'y'=4,'x'=4,'c'=2] {'x'}, dimensions={0} | all-to-all | bytes 1081344 | tf_op jit(solution)/shard_map/all_to_all | solution.py:377
  168.5 29.9 %all_to_all.26.back_ref = bf16[64,16,128]{2,1,0:T(8,128)(2,1)S(1)} all-to-all(bf16[64,16,128]{2,1,0:T(8,128)(2,1)S(1)} %shard_map.243), channel_id=1, replica_groups=mesh['z'=16,'y'=4,'x'=4,'c'=2] {'z','y'}, dimensions={0} | all-to-all | bytes 524288 | tf_op jit(solution)/shard_map/all_to_all | solution.py:386
  199.4 8.7 %all-to-all-start.4 = ((f32[8,16,128]{2,1,0:T(8,128)}), f32[8,16,128]{2,1,0:T(8,128)S(1)}, u32[]{:S(2)}, u32[]{:S(2)}) async-start(f32[8,16,128]{2,1,0:T(8,128)} %broadcast_in_dim.32), calls=%async_computation.4 | async-start | bytes 131072 | tf_op jit(solution)/shard_map/all_to_all | solution.py:397
  208.1 0.8 divide_subtract_fusion
  208.9 4.1 %all-to-all-done.4 = f32[8,16,128]{2,1,0:T(8,128)S(1)} async-done(((f32[8,16,128]{2,1,0:T(8,128)}), f32[8,16,128]{2,1,0:T(8,128)S(1)}, u32[]{:S(2)}, u32[]{:S(2)}) %all-to-all-start.4) | async-done | bytes 65568 | tf_op jit(solution)/shard_map/all_to_all | solution.py:397
  213.0 0.8 shard_map.245
  (40 shorter events, 4.7 us)
Async XLA Ops:
  7.2 129.7 %all-gather.2.cloned.1.call-start = ((), (), s32[]{:S(2)}) async-start(), calls=%async_computation.5 | async-start | bytes 7798784 | tf_op jit(solution)/shard_map/all_gather | solution.py:340
  9.4 57.4 %copy-start.10 = (bf16[1,100,4096]{2,1,0:T(8,128)(2,1)S(1)}, bf16[1,100,4096]{2,1,0:T(8,128)(2,1)}, u32[]{:S(2)}) copy-start(bf16[1,100,4096]{2,1,0:T(8,128)(2,1)} %param.24) | copy-start | bytes 2457604
  23.2 43.7 %copy-start.2 = (f32[4096]{0:T(1024)S(1)}, f32[4096]{0:T(1024)}, u32[]{:S(2)}) copy-start(f32[4096]{0:T(1024)} %param.19) | copy-start | bytes 49156
  51.2 0.9 copy-start
  52.1 0.8 copy-start.4
  54.0 28.2 %all-to-all-start = ((f32[64,8,128]{2,1,0:T(8,128)}), f32[64,8,128]{2,1,0:T(8,128)S(1)}, u32[]{:S(2)}, u32[]{:S(2)}) async-start(f32[64,8,128]{2,1,0:T(8,128)} %shard_map.241), calls=%async_computation | async-start | bytes 524288 | tf_op jit(solution)/shard_map/all_to_all | solution.py:351
  83.0 19.9 %all-to-all-start.1 = ((f32[8,8,128]{2,1,0:T(8,128)}), f32[8,8,128]{2,1,0:T(8,128)S(1)}, u32[]{:S(2)}, u32[]{:S(2)}) async-start(f32[8,8,128]{2,1,0:T(8,128)} %broadcast_in_dim.30), calls=%async_computation.1 | async-start | bytes 65536 | tf_op jit(solution)/shard_map/all_to_all | solution.py:352
  150.3 57.8 %copy-start.1 = (f32[64,512]{1,0:T(8,128)S(1)}, f32[64,512]{1,0:T(8,128)}, u32[]{:S(2)}) copy-start(f32[64,512]{1,0:T(8,128)} %col_ref.1) | copy-start | bytes 393220
  150.3 57.8 %copy-start.11 = (f32[64,512]{1,0:T(8,128)S(1)}, f32[64,512]{1,0:T(8,128)}, u32[]{:S(2)}) copy-start(f32[64,512]{1,0:T(8,128)} %param.32) | copy-start | bytes 393220
  150.3 57.7 %copy-start.12 = (f32[64,512]{1,0:T(8,128)S(1)}, f32[64,512]{1,0:T(8,128)}, u32[]{:S(2)}) copy-start(f32[64,512]{1,0:T(8,128)} %param.33) | copy-start | bytes 393220
  150.3 5.0 %collective-permute-start = (f32[4,16,4224]{2,1,0:T(8,128)S(1)}, f32[4,16,4224]{2,1,0:T(8,128)S(1)}, u32[]{:S(2)}, u32[]{:S(2)}) collective-permute-start(f32[4,16,4224]{2,1,0:T(8,128)S(1)} %get-tuple-element.28), channel_id=1, source_target_pairs={{0,1},{1,0},{2,3},{3,2},{4,5},{5,4},{6,7},{7,6},{8,9},{9,8},{10,11... | collective-permute-start | bytes 3244040 | tf_op jit(solution)/shard_map/ppermute | solution.py:376
  155.4 57.6 %copy-start.3 = (f32[100,64]{0,1:T(8,128)S(1)}, f32[100,64]{0,1:T(8,128)}, u32[]{:S(2)}) copy-start(f32[100,64]{0,1:T(8,128)} %param.25) | copy-start | bytes 76804
  155.4 57.6 %copy-start.5 = (f32[64,100]{1,0:T(8,128)S(1)}, f32[64,100]{1,0:T(8,128)}, u32[]{:S(2)}) copy-start(f32[64,100]{1,0:T(8,128)} %refs_1_.1) | copy-start | bytes 76804
  155.4 57.6 %copy-start.6 = (f32[100,64]{0,1:T(8,128)S(1)}, f32[100,64]{0,1:T(8,128)}, u32[]{:S(2)}) copy-start(f32[100,64]{0,1:T(8,128)} %param.26) | copy-start | bytes 76804
  155.4 57.6 %copy-start.7 = (f32[64,100]{1,0:T(8,128)S(1)}, f32[64,100]{1,0:T(8,128)}, u32[]{:S(2)}) copy-start(f32[64,100]{1,0:T(8,128)} %refs_3_.1) | copy-start | bytes 76804
  155.4 57.6 %copy-start.8 = (f32[100,64]{0,1:T(8,128)S(1)}, f32[100,64]{0,1:T(8,128)}, u32[]{:S(2)}) copy-start(f32[100,64]{0,1:T(8,128)} %param.27) | copy-start | bytes 76804
  155.4 57.6 %copy-start.9 = (f32[64,100]{1,0:T(8,128)S(1)}, f32[64,100]{1,0:T(8,128)}, u32[]{:S(2)}) copy-start(f32[64,100]{1,0:T(8,128)} %refs_5_.1) | copy-start | bytes 76804
  199.4 13.5 %all-to-all-start.4 = ((f32[8,16,128]{2,1,0:T(8,128)}), f32[8,16,128]{2,1,0:T(8,128)S(1)}, u32[]{:S(2)}, u32[]{:S(2)}) async-start(f32[8,16,128]{2,1,0:T(8,128)} %broadcast_in_dim.32), calls=%async_computation.4 | async-start | bytes 131072 | tf_op jit(solution)/shard_map/all_to_all | solution.py:397
Sparse Core Ops, SparseCore 0:
  23.3 113.5 all-gather.1

commit v3 on v2

--- a/solution.py
+++ b/solution.py
@@ -76,7 +76,12 @@
 
 def main_kernel(
     place_ref,
-    weight_hbm,
+    pair_hbm,
+    own_hbm,
+    left_hbm,
+    right_hbm,
+    far_first_hbm,
+    far_second_hbm,
     hidden_ref,
     up_ref,
     cols_ref,
@@ -89,7 +94,8 @@
     base_out,
     scale_out,
     line_out,
-    weights,
+    pair,
+    single,
     base,
     unit,
     normed,
@@ -103,7 +109,6 @@
     tokens = hidden_ref.shape[0]
     length = PAD + tokens
     inner = up_ref.shape[1]
-    three = 3 * inner
     depth = width // CHUNKS
     groups = cols_ref.shape[0]
     size = width // groups
@@ -111,11 +116,18 @@
     member = place_ref[0]
     core = place_ref[1]
 
+    half = single.shape[0] // 2
     copies = [
+        pltpu.make_async_copy(own_hbm, single.at[:, place_ref[2]], sems.at[0]),
+        pltpu.make_async_copy(left_hbm, single.at[:, place_ref[3]], sems.at[1]),
+        pltpu.make_async_copy(right_hbm, single.at[:, place_ref[4]], sems.at[2]),
+        pltpu.make_async_copy(far_first_hbm, single.at[:half, place_ref[5]], sems.at[3]),
+        pltpu.make_async_copy(far_second_hbm, single.at[half:, place_ref[5]], sems.at[4]),
+    ] + [
         pltpu.make_async_copy(
-            weight_hbm.at[pl.ds(k * depth, depth), :],
-            weights.at[pl.ds(k * depth, depth), :],
-            sems.at[k],
+            pair_hbm.at[pl.ds(k * depth, depth), :],
+            pair.at[pl.ds(k * depth, depth), :],
+            sems.at[5 + k],
         )
         for k in range(CHUNKS)
     ]
@@ -128,17 +140,15 @@
     rows = as_column(rows_ref[...])
     own = pl.ds(pl.multiple_of(member * BLOCK, BLOCK), BLOCK)
     squares = jnp.zeros((PAD, 1), F32)
+    for k in range(5):
+        copies[k].wait()
+    lead = single.shape[0] // CHUNKS
+    single_part = lambda k, start, stop: single[
+        k * lead : (k + 1) * lead, :, :, start:stop
+    ].reshape(depth, stop - start)
     for k in range(CHUNKS):
-        copies[k].wait()
         span = slice(k * depth, (k + 1) * depth)
-        part = dot(hidden_ref[:, span], weights[span, :three], 1, 0)
-        if k == 0:
-            total[...] = part
-        elif k < CHUNKS - 1:
-            total[...] += part
-        else:
-            qkv[PAD:, :] = (total[...] + part).astype(BF16)
-        base_part = jnp.transpose(weights[span, three:].astype(F32))
+        base_part = jnp.transpose(single_part(k, inner, inner + LANES).astype(F32))
         base[:, span] = base_part
         act = (base_part * rows * line[:, span]).astype(BF16).astype(F32)
         unit[:, span] = act
@@ -152,7 +162,20 @@
         unit_part = unit[:, span] * inverse
         unit[:, span] = unit_part
         normed[:, span] = (unit_part * gain_ref[:, span]).astype(BF16)
-    qkv[:PAD, :] = dot(normed[...], weights[:, :three], 1, 0).astype(BF16)
+    query_weights = single[:, :, :, :inner].reshape(width, inner)
+    qkv[PAD:, :inner] = dot(hidden_ref[...], query_weights, 1, 0).astype(BF16)
+    qkv[:PAD, :inner] = dot(normed[...], query_weights, 1, 0).astype(BF16)
+    for k in range(CHUNKS):
+        copies[5 + k].wait()
+        span = slice(k * depth, (k + 1) * depth)
+        part = dot(hidden_ref[:, span], pair[span, :], 1, 0)
+        if k == 0:
+            total[...] = part
+        elif k < CHUNKS - 1:
+            total[...] += part
+        else:
+            qkv[PAD:, inner:] = (total[...] + part).astype(BF16)
+    qkv[:PAD, inner:] = dot(normed[...], pair[...], 1, 0).astype(BF16)
 
     column = iota((length, length), 1)
     real_key = (column < PROMPT) | (column >= PAD)
@@ -185,7 +208,9 @@
     strength = inverse * rows
     for g in range(groups):
         span = slice(g * size, (g + 1) * size)
-        part = dot(grad_all, weights[span, :three], 1, 1)
+        place = slice(g * single.shape[0] // groups, (g + 1) * single.shape[0] // groups)
+        part = dot(grad_all[:, :inner], single[place, :, :, :inner].reshape(size, inner), 1, 1)
+        part = part + dot(grad_all[:, inner:], pair[span, :], 1, 1)
         parts[:, span] = part
         weighted = base[:, span] * strength
         base_own = base[own, span]
@@ -210,10 +235,11 @@
         send_ref[pair, :, :] = parts[pl.ds(start, BLOCK), :]
 
 
-def main_part(place, weights, hidden, up, cols, rows, gain, cot):
+def main_part(place, pair, singles, hidden, up, cols, rows, gain, cot):
     width = hidden.shape[1]
     length = PAD + hidden.shape[0]
-    three = 3 * up.shape[1]
+    inner = up.shape[1]
+    ring = width // (singles[0].shape[0] * singles[0].shape[1])
     groups = cols.shape[0]
     half = jax.ShapeDtypeStruct((groups // 2, BLOCK, width + LANES), F32)
     own = jax.ShapeDtypeStruct((BLOCK, width), F32)
@@ -227,21 +253,22 @@
             jax.ShapeDtypeStruct((BLOCK, LANES), F32),
             jax.ShapeDtypeStruct((1, width), F32),
         ),
-        in_specs=[SMEM, pl.BlockSpec(memory_space=pl.ANY)] + [VMEM] * 6,
+        in_specs=[SMEM] + [pl.BlockSpec(memory_space=pl.ANY)] * 6 + [VMEM] * 6,
         out_specs=(VMEM,) * 6,
         scratch_shapes=[
-            pltpu.VMEM(weights.shape, BF16),
+            pltpu.VMEM(pair.shape, BF16),
+            pltpu.VMEM((singles[0].shape[0], ring) + singles[0].shape[1:], BF16),
             pltpu.VMEM((PAD, width), F32),
             pltpu.VMEM((PAD, width), F32),
             pltpu.VMEM((PAD, width), BF16),
-            pltpu.VMEM((length - PAD, three), F32),
-            pltpu.VMEM((length, three), BF16),
+            pltpu.VMEM((length - PAD, 2 * inner), F32),
+            pltpu.VMEM((length, 3 * inner), BF16),
             pltpu.VMEM((PAD, width + LANES), F32),
             pltpu.VMEM((PAD, LANES), F32),
-            pltpu.SemaphoreType.DMA((CHUNKS,)),
+            pltpu.SemaphoreType.DMA((5 + CHUNKS,)),
         ],
         compiler_params=PARAMS,
-    )(place, weights, hidden, up, cols, rows, gain, cot)
+    )(place, pair, *singles, hidden, up, cols, rows, gain, cot)
 
 
 def prompt_kernel(pieces, got_ref, unit_ref, base_ref, cot_ref, gain_ref, cols_ref, scale_ref, out_ref):
@@ -329,17 +356,36 @@
     owned, col_width = col_factor.shape
     width = hidden_rows.shape[2]
     pieces = col_width // LANES
-    padding = ((0, 0), (0, LANES - PROMPT))
-
-    weights = jnp.concatenate(
-        [w_query, w_key, w_value, jnp.pad(prompt_master.T.astype(BF16), padding)], axis=1
-    )
-    weights = lax.all_gather(weights, "y", axis=0, tiled=True)
+
+    depth = w_query.shape[0]
+    inner = w_query.shape[1]
+    ring = lax.axis_size("y")
     slot = lax.dynamic_index_in_dim(tenant_slot, row_tenant[0], 0, keepdims=False)
-    weights, slot = lax.optimization_barrier((weights, slot))
-    weights = lax.all_gather(weights, "z", axis=0, tiled=True)
-
-    slots = lax.psum(jnp.where(lax.iota(jnp.int32, count) == device, slot, 0), dp)[None, :]
+    marks = jnp.stack([slot // owned, slot % owned]).astype(BF16)
+    marks = jnp.broadcast_to(jnp.pad(marks, (0, LANES - 2))[None], (depth, LANES))
+    pair = lax.all_gather(jnp.concatenate([w_key, w_value, marks], axis=1), "y", axis=0, tiled=True)
+    marks = pair.reshape(ring, depth, -1)[:, 0, 2 * inner : 2 * inner + 2].reshape(-1)
+    pair = pair[:, : 2 * inner]
+
+    marks = jnp.broadcast_to(
+        jnp.pad(marks, (0, LANES - PROMPT - marks.shape[0]))[None], (depth, LANES - PROMPT)
+    )
+    own = jnp.concatenate([w_query, prompt_master.T.astype(BF16), marks], axis=1)
+    pair, own = lax.optimization_barrier((pair, own))
+    pair = lax.all_gather(pair, "z", axis=0, tiled=True)
+    own = lax.all_gather(own, "z", axis=0, tiled=False)
+    half = own.shape[0] // 2
+    up_ring = [(i, (i + 1) % ring) for i in range(ring)]
+    down_ring = [(i, (i - 1) % ring) for i in range(ring)]
+    left = lax.ppermute(own, "y", up_ring)
+    right = lax.ppermute(own, "y", down_ring)
+    far_first = lax.ppermute(left[:half], "y", up_ring)
+    far_second = lax.ppermute(right[half:], "y", down_ring)
+    singles = (own, left, right, far_first, far_second)
+
+    marks = own[:, 0, inner + PROMPT : inner + PROMPT + 2 * ring].reshape(count, 2)
+    marks = marks.astype(jnp.int32)
+    slots = (marks[:, 0] * owned + marks[:, 1])[None, :]
     first = (device * owned).astype(jnp.int32).reshape(1)
     terms = pl.pallas_call(
         factor_kernel,
@@ -368,9 +414,12 @@
     cot = lax.dynamic_slice_in_dim(
         jnp.pad(prompt_cotangent[0], ((0, PAD - PROMPT), (0, 0))), member * BLOCK, BLOCK, 0
     )
-    place = jnp.stack([member, lax.axis_index("c")]).astype(jnp.int32)
+    y = lax.axis_index("y")
+    place = jnp.stack(
+        [member, lax.axis_index("c"), y, (y - 1) % ring, (y + 1) % ring, (y + 2) % ring]
+    ).astype(jnp.int32)
     keep, send, unit_own, base_own, scale_own, line = main_part(
-        place, weights, hidden, upstream, factor_cols, factor_rows, gain, cot
+        place, pair, singles, hidden, upstream, factor_cols, factor_rows, gain, cot
     )
 
     parts = (keep + lax.ppermute(send, "c", [(0, 1), (1, 0)])).astype(BF16)

time: 222 us -> 211 us (0.950)
  waiting for transfers between devices: 55.8 us -> 14.5 us
  starting transfers between devices: 34.9 us -> 48.7 us
  blocking collectives: 82.3 us -> 90 us
  local copies, waits for them, and re-layouts: 6.1 us -> 9.78 us
  between operations: 14.9 us -> 17.6 us
  Pallas kernels: 16.1 us -> 18.6 us
    all_gather x1 -> x2, blocking collectives: 12.4 us -> 49.2 us  [the longest x1 38.4 us: local(): own = lax.all_gather(own, 'z', axis=0, tiled=False)]
    all_gather x1, waiting for transfers between devices: 34 us -> 0.01 us  [local(): pair = lax.all_gather(pair, 'z', axis=0, tiled=True)]
    psum x1 -> x0, blocking collectives: 27.4 us -> none  [local(): lax.psum(jnp.where(lax.iota(jnp.int32, count) == device, slot, 0), dp)]
    ppermute x0 -> x4, starting transfers between devices: none -> 11.3 us  [the longest x1 4.12 us: local(): far_second = lax.ppermute(right[half:], 'y', down_ring)]
    all_to_all x1, waiting for transfers between devices: 10.7 us -> 3.31 us  [local(): terms = jnp.sum(lax.all_to_all(terms, dp, 0, 0, tiled=False), axis=0)]
    all_to_all x1, starting transfers between devices: 15.1 us -> 19 us  [local(): lax.all_to_all(jnp.broadcast_to(terms[None], (groups, 8, LANES)), mp, 0,...]
    pallas_call x1, Pallas kernels: 13.4 us -> 15.8 us  [main_part(): pl.pallas_call(main_kernel, out_shape=(half, half, own, own, jax.ShapeDty...]
  transfers between devices with their start and end apart: 5 -> 9, of which waited for: 5 -> 4; matrix products, arithmetic and copies ran while one was open for 5% -> 5% of each run, Pallas kernels for 1% -> 1%
where the time goes in v3:
time: 211 us; the launch traced here: 210 us
  blocking collectives  90 us (43%)
  starting transfers between devices  48.7 us (23%)
  Pallas kernels  18.6 us (9%)
  between operations  17.6 us (8%)
  waiting for transfers between devices  14.5 us (7%)
  other arithmetic  10.5 us (5%)
  local copies, waits for them, and re-layouts  9.78 us (5%)
    all_gather x1, blocking collectives, local(): own = lax.all_gather(own, 'z', axis=0, tiled=False)  38.4 us
    all_to_all x1, blocking collectives, local(): back = lax.all_to_all(outgoing, dp, 0, 0, tiled=False)  29 us
    all_to_all x1, starting transfers between devices, local(): lax.all_to_all(jnp.broadcast_to(terms[None], (groups, 8, LANES)), mp, 0,...  19 us
    pallas_call x1, Pallas kernels, main_part(): pl.pallas_call(main_kernel, out_shape=(half, half, own, own, jax.ShapeDty...  15.8 us
    all_to_all x1, blocking collectives, local(): parts = lax.all_to_all(parts, 'x', 0, 0, tiled=False)  11.8 us
    all_gather x1, blocking collectives, local(): lax.all_gather(jnp.concatenate([w_key, w_value, marks], axis=1), 'y', axi...  10.9 us
    all_to_all x1, starting transfers between devices, local(): lax.all_to_all(jnp.broadcast_to(shared[None], (groups, BLOCK, LANES)), mp...  8.31 us
    all_to_all x1, starting transfers between devices, local(): terms = jnp.sum(lax.all_to_all(terms, dp, 0, 0, tiled=False), axis=0)  7.28 us
  transfers between devices with their start and end apart: 9, of which 4 were waited for; matrix products, arithmetic and copies ran while one was open for 5% of the time, Pallas kernels for 1%

profile of v3, /device:TPU:1, one launch (start us, length us, event | category | flops | bytes accessed | tf_op | source)
XLA Modules:
  0.0 209.7 jit_solution(9835998139158244078)
XLA Ops:
  7.9 1.3 dynamic_slice.7
  13.4 10.9 %all_gather.12 = bf16[256,640]{1,0:T(8,128)(2,1)S(1)} all-gather(bf16[64,640]{1,0:T(8,128)(2,1)S(1)} %maximum_maximum_fusion), channel_id=1, replica_groups=mesh['z'=16,'y'=4,'x'=4,'c'=2] {'y'}, dimensions={0}, use_global_device_ids=true | all-gather | bytes 409600 | tf_op jit(solution)/shard_map/all_gather | solution.py:366
  26.0 38.4 %all-gather = bf16[1024,384]{1,0:T(8,128)(2,1)S(1)} all-gather(bf16[64,384]{1,0:T(8,128)(2,1)S(1)} %maximum_maximum_fusion.1), channel_id=2, replica_groups=mesh['z'=16,'y'=4,'x'=4,'c'=2] {'z'}, dimensions={0}, use_global_device_ids=true | all-gather | bytes 835584 | tf_op jit(solution)/shard_map/all_gather | solution.py:376
  64.4 1.9 collective-permute-start.1
  66.3 3.4 %collective-permute-start = (bf16[16,64,384]{2,1,0:T(8,128)(2,1)S(1)}, bf16[16,64,384]{2,1,0:T(8,128)(2,1)S(1)}, u32[]{:S(2)}, u32[]{:S(2)}) collective-permute-start(bf16[16,64,384]{2,1,0:T(8,128)(2,1)S(1)} %bitcast.36), channel_id=1, source_target_pairs={{0,8},{8,16},{16,24},{24,0},{1,9},{9,17},{17,25},{25,1},{2,10},{10... | collective-permute-start | bytes 2359304 | tf_op jit(solution)/shard_map/ppermute | solution.py:380
  71.7 1.2 shard_map.241
  72.9 7.3 %all-to-all-start = ((f32[64,8,128]{2,1,0:T(8,128)}), f32[64,8,128]{2,1,0:T(8,128)S(1)}, u32[]{:S(2)}, u32[]{:S(2)}) async-start(f32[64,8,128]{2,1,0:T(8,128)} %shard_map.241), calls=%async_computation | async-start | bytes 524288 | tf_op jit(solution)/shard_map/all_to_all | solution.py:397
  80.2 2.8 %fusion = f32[384]{0:T(512)S(1)} fusion(bf16[1,384,4096]{2,1,0:T(8,128)(2,1)} %param.18), kind=kLoop, calls=%fused_computation.2 | loop fusion | flops 4718208 | bytes 3147264 | tf_op jit(solution)/shard_map/reduce_sum | solution.py:405
  83.1 2.7 %fusion.2.hidden_ref = bf16[384,4096]{1,0:T(8,128)(2,1)} fusion(bf16[1,384,4096]{2,1,0:T(8,128)(2,1)S(1)} %copy-done.10, f32[4096]{0:T(1024)S(1)} %copy-done.2, f32[384]{0:T(512)S(1)} %add_rsqrt_fusion), kind=kLoop, calls=%fused_computation.4 | loop fusion | flops 6291456 | bytes 6309376 | tf_op jit(solution)/shard_map/convert_element_type | solution.py:406
  85.8 0.9 pad_dynamic-slice_fusion.cot_ref.refs_3_
  87.7 4.1 %collective-permute-start.3 = (bf16[8,64,384]{2,1,0:T(8,128)(2,1)S(1)}, bf16[8,64,384]{2,1,0:T(8,128)(2,1)S(1)}, u32[]{:S(2)}, u32[]{:S(2)}) collective-permute-start(bf16[8,64,384]{2,1,0:T(8,128)(2,1)S(1)} %slice.46), channel_id=1, source_target_pairs={{0,24},{8,0},{16,8},{24,16},{1,25},{9,1},{17,9},{25,17},{2,26},{10... | collective-permute-start | bytes 1179656 | tf_op jit(solution)/shard_map/ppermute | solution.py:383
  92.6 1.9 collective-permute-start.2
  95.3 1.0 slice_bitcast_fusion
  96.3 3.3 %all-to-all-done = f32[64,8,128]{2,1,0:T(8,128)S(1)} async-done(((f32[64,8,128]{2,1,0:T(8,128)}), f32[64,8,128]{2,1,0:T(8,128)S(1)}, u32[]{:S(2)}, u32[]{:S(2)}) %all-to-all-start) | async-done | bytes 262176 | tf_op jit(solution)/shard_map/all_to_all | solution.py:397
  100.3 19.0 %all-to-all-start.1 = ((f32[8,8,128]{2,1,0:T(8,128)}), f32[8,8,128]{2,1,0:T(8,128)S(1)}, u32[]{:S(2)}, u32[]{:S(2)}) async-start(f32[8,8,128]{2,1,0:T(8,128)} %broadcast_in_dim.12), calls=%async_computation.1 | async-start | bytes 65536 | tf_op jit(solution)/shard_map/all_to_all | solution.py:398
  119.4 4.6 %all-to-all-done.1.cols_ref = f32[8,8,128]{2,1,0:T(8,128)S(1)} async-done(((f32[8,8,128]{2,1,0:T(8,128)}), f32[8,8,128]{2,1,0:T(8,128)S(1)}, u32[]{:S(2)}, u32[]{:S(2)}) %all-to-all-start.1) | async-done | bytes 32800 | tf_op jit(solution)/shard_map/all_to_all | solution.py:398
  124.0 15.8 %shard_map.242 = (f32[4,16,4224]{2,1,0:T(8,128)}, f32[4,16,4224]{2,1,0:T(8,128)}, f32[16,4096]{1,0:T(8,128)S(1)}, f32[16,4096]{1,0:T(8,128)S(1)}, f32[16,128]{1,0:T(8,128)S(1)}, /*index=5*/f32[1,4096]{1,0:T(1,128)S(1)}) custom-call(s32[6]{0:T(128)S(1)} %stack.42.place_ref, bf16[4096,512]{1,0:T(8,128)(2,1)} %all-gather.3.cloned.1.call-done.pair_hbm, ...), custom_call_target="tpu_custom_call" | custom-call | tf_op jit(solution)/shard_map/pallas_call | solution.py:246
  139.9 2.8 %collective-permute-start.4 = (f32[4,16,4224]{2,1,0:T(8,128)}, f32[4,16,4224]{2,1,0:T(8,128)S(1)}, u32[]{:S(2)}, u32[]{:S(2)}) collective-permute-start(f32[4,16,4224]{2,1,0:T(8,128)} %get-tuple-element.28), channel_id=1, source_target_pairs={{0,1},{1,0},{2,3},{3,2},{4,5},{5,4},{6,7},{7,6},{8,9},{9,8},{10,11... | collective-permute-start | bytes 3244040 | tf_op jit(solution)/shard_map/ppermute | solution.py:425
  142.6 2.5 %collective-permute-done.4 = f32[4,16,4224]{2,1,0:T(8,128)S(1)} collective-permute-done((f32[4,16,4224]{2,1,0:T(8,128)}, f32[4,16,4224]{2,1,0:T(8,128)S(1)}, u32[]{:S(2)}, u32[]{:S(2)}) %collective-permute-start.4) | collective-permute-done | bytes 1081376 | tf_op jit(solution)/shard_map/ppermute | solution.py:425
  145.2 1.4 add_convert_fusion
  146.6 11.8 %all_to_all.25.refs_0_ = bf16[4,16,4224]{2,1,0:T(8,128)(2,1)S(1)} all-to-all(bf16[4,16,4224]{2,1,0:T(8,128)(2,1)S(1)} %add_convert_fusion), channel_id=1, replica_groups=mesh['z'=16,'y'=4,'x'=4,'c'=2] {'x'}, dimensions={0} | all-to-all | bytes 1081344 | tf_op jit(solution)/shard_map/all_to_all | solution.py:426
  158.7 29.0 %all_to_all.26.back_ref = bf16[64,16,128]{2,1,0:T(8,128)(2,1)S(1)} all-to-all(bf16[64,16,128]{2,1,0:T(8,128)(2,1)S(1)} %shard_map.243), channel_id=1, replica_groups=mesh['z'=16,'y'=4,'x'=4,'c'=2] {'z','y'}, dimensions={0} | all-to-all | bytes 524288 | tf_op jit(solution)/shard_map/all_to_all | solution.py:435
  188.8 8.3 %all-to-all-start.4 = ((f32[8,16,128]{2,1,0:T(8,128)}), f32[8,16,128]{2,1,0:T(8,128)S(1)}, u32[]{:S(2)}, u32[]{:S(2)}) async-start(f32[8,16,128]{2,1,0:T(8,128)} %broadcast_in_dim.14), calls=%async_computation.4 | async-start | bytes 131072 | tf_op jit(solution)/shard_map/all_to_all | solution.py:446
  197.9 4.1 %all-to-all-done.4 = f32[8,16,128]{2,1,0:T(8,128)S(1)} async-done(((f32[8,16,128]{2,1,0:T(8,128)}), f32[8,16,128]{2,1,0:T(8,128)S(1)}, u32[]{:S(2)}, u32[]{:S(2)}) %all-to-all-start.4) | async-done | bytes 65568 | tf_op jit(solution)/shard_map/all_to_all | solution.py:446
  (61 shorter events, 11.9 us)
Async XLA Ops:
  7.2 116.8 %all-gather.3.cloned.1.call-start = ((), (), s32[]{:S(2)}) async-start(), calls=%async_computation.5 | async-start | bytes 4456448 | tf_op jit(solution)/shard_map/all_gather | solution.py:375
  13.4 69.5 %copy-start.2 = (f32[4096]{0:T(1024)S(1)}, f32[4096]{0:T(1024)}, u32[]{:S(2)}) copy-start(f32[4096]{0:T(1024)} %param.19) | copy-start | bytes 49156
  64.4 22.4 %collective-permute-start.1 = (bf16[16,64,384]{2,1,0:T(8,128)(2,1)S(1)}, bf16[16,64,384]{2,1,0:T(8,128)(2,1)S(1)}, u32[]{:S(2)}, u32[]{:S(2)}) collective-permute-start(bf16[16,64,384]{2,1,0:T(8,128)(2,1)S(1)} %bitcast.35), channel_id=1, source_target_pairs={{0,24},{8,0},{16,8},{24,16},{1,25},{9,1},{17,9},{25,17},{2,26},{10... | collective-permute-start | bytes 2359304 | tf_op jit(solution)/shard_map/ppermute | solution.py:381
  66.3 25.5 %collective-permute-start = (bf16[16,64,384]{2,1,0:T(8,128)(2,1)S(1)}, bf16[16,64,384]{2,1,0:T(8,128)(2,1)S(1)}, u32[]{:S(2)}, u32[]{:S(2)}) collective-permute-start(bf16[16,64,384]{2,1,0:T(8,128)(2,1)S(1)} %bitcast.36), channel_id=1, source_target_pairs={{0,8},{8,16},{16,24},{24,0},{1,9},{9,17},{17,25},{25,1},{2,10},{10... | collective-permute-start | bytes 2359304 | tf_op jit(solution)/shard_map/ppermute | solution.py:380
  70.0 0.9 copy-start
  70.9 0.8 copy-start.4
  72.9 26.7 %all-to-all-start = ((f32[64,8,128]{2,1,0:T(8,128)}), f32[64,8,128]{2,1,0:T(8,128)S(1)}, u32[]{:S(2)}, u32[]{:S(2)}) async-start(f32[64,8,128]{2,1,0:T(8,128)} %shard_map.241), calls=%async_computation | async-start | bytes 524288 | tf_op jit(solution)/shard_map/all_to_all | solution.py:397
  80.2 2.9 %copy-start.10 = (bf16[1,384,4096]{2,1,0:T(8,128)(2,1)S(1)}, bf16[1,384,4096]{2,1,0:T(8,128)(2,1)}, u32[]{:S(2)}) copy-start(bf16[1,384,4096]{2,1,0:T(8,128)(2,1)} %param.18) | copy-start | bytes 9437188
  86.7 0.9 copy-start.11
  87.7 36.3 %collective-permute-start.3 = (bf16[8,64,384]{2,1,0:T(8,128)(2,1)S(1)}, bf16[8,64,384]{2,1,0:T(8,128)(2,1)S(1)}, u32[]{:S(2)}, u32[]{:S(2)}) collective-permute-start(bf16[8,64,384]{2,1,0:T(8,128)(2,1)S(1)} %slice.46), channel_id=1, source_target_pairs={{0,24},{8,0},{16,8},{24,16},{1,25},{9,1},{17,9},{25,17},{2,26},{10... | collective-permute-start | bytes 1179656 | tf_op jit(solution)/shard_map/ppermute | solution.py:383
  92.6 31.4 %collective-permute-start.2 = (bf16[8,64,384]{2,1,0:T(8,128)(2,1)}, bf16[8,64,384]{2,1,0:T(8,128)(2,1)S(1)}, u32[]{:S(2)}, u32[]{:S(2)}) collective-permute-start(bf16[8,64,384]{2,1,0:T(8,128)(2,1)} %slice.45), channel_id=1, source_target_pairs={{0,8},{8,16},{16,24},{24,0},{1,9},{9,17},{17,25},{25,1},{2,10},{10... | collective-permute-start | bytes 1179656 | tf_op jit(solution)/shard_map/ppermute | solution.py:382
  100.3 23.7 %all-to-all-start.1 = ((f32[8,8,128]{2,1,0:T(8,128)}), f32[8,8,128]{2,1,0:T(8,128)S(1)}, u32[]{:S(2)}, u32[]{:S(2)}) async-start(f32[8,8,128]{2,1,0:T(8,128)} %broadcast_in_dim.12), calls=%async_computation.1 | async-start | bytes 65536 | tf_op jit(solution)/shard_map/all_to_all | solution.py:398
  139.8 57.3 %copy-start.1 = (f32[64,512]{1,0:T(8,128)S(1)}, f32[64,512]{1,0:T(8,128)}, u32[]{:S(2)}) copy-start(f32[64,512]{1,0:T(8,128)} %col_ref.1) | copy-start | bytes 393220
  139.8 57.3 %copy-start.12 = (f32[64,512]{1,0:T(8,128)S(1)}, f32[64,512]{1,0:T(8,128)}, u32[]{:S(2)}) copy-start(f32[64,512]{1,0:T(8,128)} %param.32) | copy-start | bytes 393220
  139.9 57.3 %copy-start.13 = (f32[64,512]{1,0:T(8,128)S(1)}, f32[64,512]{1,0:T(8,128)}, u32[]{:S(2)}) copy-start(f32[64,512]{1,0:T(8,128)} %param.33) | copy-start | bytes 393220
  139.9 5.3 %collective-permute-start.4 = (f32[4,16,4224]{2,1,0:T(8,128)}, f32[4,16,4224]{2,1,0:T(8,128)S(1)}, u32[]{:S(2)}, u32[]{:S(2)}) collective-permute-start(f32[4,16,4224]{2,1,0:T(8,128)} %get-tuple-element.28), channel_id=1, source_target_pairs={{0,1},{1,0},{2,3},{3,2},{4,5},{5,4},{6,7},{7,6},{8,9},{9,8},{10,11... | collective-permute-start | bytes 3244040 | tf_op jit(solution)/shard_map/ppermute | solution.py:425
  145.2 56.8 %copy-start.3 = (f32[100,64]{0,1:T(8,128)S(1)}, f32[100,64]{0,1:T(8,128)}, u32[]{:S(2)}) copy-start(f32[100,64]{0,1:T(8,128)} %param.25) | copy-start | bytes 76804
  145.2 56.8 %copy-start.5 = (f32[64,100]{1,0:T(8,128)S(1)}, f32[64,100]{1,0:T(8,128)}, u32[]{:S(2)}) copy-start(f32[64,100]{1,0:T(8,128)} %refs_1_.1) | copy-start | bytes 76804
  145.2 56.8 %copy-start.6 = (f32[100,64]{0,1:T(8,128)S(1)}, f32[100,64]{0,1:T(8,128)}, u32[]{:S(2)}) copy-start(f32[100,64]{0,1:T(8,128)} %param.26) | copy-start | bytes 76804
  145.2 56.8 %copy-start.7 = (f32[64,100]{1,0:T(8,128)S(1)}, f32[64,100]{1,0:T(8,128)}, u32[]{:S(2)}) copy-start(f32[64,100]{1,0:T(8,128)} %refs_3_.1) | copy-start | bytes 76804
  145.2 56.8 %copy-start.8 = (f32[100,64]{0,1:T(8,128)S(1)}, f32[100,64]{0,1:T(8,128)}, u32[]{:S(2)}) copy-start(f32[100,64]{0,1:T(8,128)} %param.27) | copy-start | bytes 76804
  145.2 56.8 %copy-start.9 = (f32[64,100]{1,0:T(8,128)S(1)}, f32[64,100]{1,0:T(8,128)}, u32[]{:S(2)}) copy-start(f32[64,100]{1,0:T(8,128)} %refs_5_.1) | copy-start | bytes 76804
  188.8 13.2 %all-to-all-start.4 = ((f32[8,16,128]{2,1,0:T(8,128)}), f32[8,16,128]{2,1,0:T(8,128)S(1)}, u32[]{:S(2)}, u32[]{:S(2)}) async-start(f32[8,16,128]{2,1,0:T(8,128)} %broadcast_in_dim.14), calls=%async_computation.4 | async-start | bytes 131072 | tf_op jit(solution)/shard_map/all_to_all | solution.py:446
Sparse Core Ops, SparseCore 0:
  26.1 88.9 all-gather.2

commit v4 on v3

--- a/solution.py
+++ b/solution.py
@@ -25,7 +25,8 @@
 F32 = jnp.float32
 VMEM = pl.BlockSpec(memory_space=pltpu.VMEM)
 SMEM = pl.BlockSpec(memory_space=pltpu.SMEM)
-PARAMS = pltpu.CompilerParams(vmem_limit_bytes=50 * 1024 * 1024)
+PARAMS = pltpu.CompilerParams(vmem_limit_bytes=16 * 1024 * 1024)
+MAIN_PARAMS = pltpu.CompilerParams(vmem_limit_bytes=32 * 1024 * 1024)
 
 
 def adam_step(param, moment_one, moment_two, gradient):
@@ -56,6 +57,17 @@
     size = line.shape[1]
     eye = iota((size, size), 0) == iota((size, size), 1)
     return jnp.sum(jnp.where(eye, line, 0.0), axis=1, keepdims=True)
+
+
+def lead_kernel(owned, tenant_ref, slot_ref, key_ref, value_ref, out_ref):
+    depth, inner = key_ref.shape
+    slot = slot_ref[tenant_ref[0]]
+    owner = lax.div(slot, owned)
+    lane = iota((depth, LANES), 1)
+    marks = jnp.where(lane == 0, owner, jnp.where(lane == 1, slot - owner * owned, 0))
+    out_ref[:, :inner] = key_ref[...]
+    out_ref[:, inner : 2 * inner] = value_ref[...]
+    out_ref[:, 2 * inner :] = marks.astype(F32).astype(BF16)
 
 
 def factor_kernel(first_ref, slot_ref, row_ref, col_ref, out_ref):
@@ -99,7 +111,6 @@
     base,
     unit,
     normed,
-    total,
     qkv,
     parts,
     scale,
@@ -167,14 +178,7 @@
     qkv[:PAD, :inner] = dot(normed[...], query_weights, 1, 0).astype(BF16)
     for k in range(CHUNKS):
         copies[5 + k].wait()
-        span = slice(k * depth, (k + 1) * depth)
-        part = dot(hidden_ref[:, span], pair[span, :], 1, 0)
-        if k == 0:
-            total[...] = part
-        elif k < CHUNKS - 1:
-            total[...] += part
-        else:
-            qkv[PAD:, inner:] = (total[...] + part).astype(BF16)
+    qkv[PAD:, inner:] = dot(hidden_ref[...], pair[...], 1, 0).astype(BF16)
     qkv[:PAD, inner:] = dot(normed[...], pair[...], 1, 0).astype(BF16)
 
     column = iota((length, length), 1)
@@ -253,7 +257,9 @@
             jax.ShapeDtypeStruct((BLOCK, LANES), F32),
             jax.ShapeDtypeStruct((1, width), F32),
         ),
-        in_specs=[SMEM] + [pl.BlockSpec(memory_space=pl.ANY)] * 6 + [VMEM] * 6,
+        in_specs=[SMEM, pl.BlockSpec(memory_space=pltpu.HBM)]
+        + [pl.BlockSpec(memory_space=pl.ANY)] * 5
+        + [VMEM] * 6,
         out_specs=(VMEM,) * 6,
         scratch_shapes=[
             pltpu.VMEM(pair.shape, BF16),
@@ -261,13 +267,12 @@
             pltpu.VMEM((PAD, width), F32),
             pltpu.VMEM((PAD, width), F32),
             pltpu.VMEM((PAD, width), BF16),
-            pltpu.VMEM((length - PAD, 2 * inner), F32),
             pltpu.VMEM((length, 3 * inner), BF16),
             pltpu.VMEM((PAD, width + LANES), F32),
             pltpu.VMEM((PAD, LANES), F32),
             pltpu.SemaphoreType.DMA((5 + CHUNKS,)),
         ],
-        compiler_params=PARAMS,
+        compiler_params=MAIN_PARAMS,
     )(place, pair, *singles, hidden, up, cols, rows, gain, cot)
 
 
@@ -316,7 +321,8 @@
             first_half, swap_halves(lower), upper
         )
     rows = dot(back[:, 2 * pieces, :].astype(BF16), picker, 0, 1)
-    shared_ref[...] = jnp.concatenate([total[:, :HALF], rows[HALF : HALF + BLOCK, :]], axis=1)
+    shared = jnp.concatenate([total[:, :HALF], rows[HALF : HALF + BLOCK, :]], axis=1)
+    shared_ref[...] = jnp.broadcast_to(shared[None], shared_ref.shape)
 
 
 def update_kernel(grads_ref, *refs):
@@ -360,10 +366,14 @@
     depth = w_query.shape[0]
     inner = w_query.shape[1]
     ring = lax.axis_size("y")
-    slot = lax.dynamic_index_in_dim(tenant_slot, row_tenant[0], 0, keepdims=False)
-    marks = jnp.stack([slot // owned, slot % owned]).astype(BF16)
-    marks = jnp.broadcast_to(jnp.pad(marks, (0, LANES - 2))[None], (depth, LANES))
-    pair = lax.all_gather(jnp.concatenate([w_key, w_value, marks], axis=1), "y", axis=0, tiled=True)
+    pair = pl.pallas_call(
+        lambda *refs: lead_kernel(owned, *refs),
+        out_shape=jax.ShapeDtypeStruct((depth, 2 * inner + LANES), BF16),
+        in_specs=[SMEM, SMEM, VMEM, VMEM],
+        out_specs=VMEM,
+        compiler_params=PARAMS,
+    )(row_tenant, tenant_slot, w_key, w_value)
+    pair = lax.all_gather(pair, "y", axis=0, tiled=True)
     marks = pair.reshape(ring, depth, -1)[:, 0, 2 * inner : 2 * inner + 2].reshape(-1)
     pair = pair[:, : 2 * inner]
 
@@ -436,16 +446,14 @@
     shared, col_grad = pl.pallas_call(
         owner_kernel,
         out_shape=(
-            jax.ShapeDtypeStruct((BLOCK, LANES), F32),
+            jax.ShapeDtypeStruct((groups, BLOCK, LANES), F32),
             jax.ShapeDtypeStruct((owned, col_width), F32),
         ),
         in_specs=[SMEM, VMEM, VMEM],
         out_specs=(VMEM, VMEM),
         compiler_params=PARAMS,
     )(first, slots, back)
-    shared = lax.all_to_all(
-        jnp.broadcast_to(shared[None], (groups, BLOCK, LANES)), mp, 0, 0, tiled=False
-    ).reshape(PAD, LANES)
+    shared = lax.all_to_all(shared, mp, 0, 0, tiled=False).reshape(PAD, LANES)
     operands = [
         part
         for pair in zip(

time: 211 us -> 215 us (1.019)
  local copies, waits for them, and re-layouts: 9.78 us -> 19.9 us
  waiting for transfers between devices: 14.5 us -> 10.2 us
  blocking collectives: 90 us -> 94.3 us
  between operations: 17.6 us -> 15 us
    unnamed x28 -> x42, local copies, waits for them, and re-layouts: 2.69 us -> 8.1 us
    pallas_call x1, Pallas kernels: 15.8 us -> 12.7 us  [main_part(): pl.pallas_call(main_kernel, out_shape=(half, half, own, own, jax.ShapeDty...]
    all_to_all x1, waiting for transfers between devices: 4.57 us -> 1.92 us  [local(): lax.all_to_all(jnp.broadcast_to(terms[None], (groups, 8, LANES)), mp, 0,...]
    all_to_all x1, blocking collectives: 29 us -> 31.2 us  [local(): back = lax.all_to_all(outgoing, dp, 0, 0, tiled=False)]
  transfers between devices with their start and end apart: 9 -> 9, of which waited for: 4 -> 4; matrix products, arithmetic and copies ran while one was open for 5% -> 9% of each run, Pallas kernels for 1% -> 1%
where the time goes in v4:
time: 215 us; the launch traced here: 213 us
  blocking collectives  94.3 us (44%)
  starting transfers between devices  47.6 us (22%)
  local copies, waits for them, and re-layouts  19.9 us (9%)
  Pallas kernels  16.8 us (8%)
  between operations  15 us (7%)
  waiting for transfers between devices  10.2 us (5%)
  other arithmetic  9.12 us (4%)
    all_gather x1, blocking collectives, local(): own = lax.all_gather(own, 'z', axis=0, tiled=False)  40.5 us
    all_to_all x1, blocking collectives, local(): back = lax.all_to_all(outgoing, dp, 0, 0, tiled=False)  31.2 us
    all_to_all x1, starting transfers between devices, local(): lax.all_to_all(jnp.broadcast_to(terms[None], (groups, 8, LANES)), mp, 0,...  18 us
    pallas_call x1, Pallas kernels, main_part(): pl.pallas_call(main_kernel, out_shape=(half, half, own, own, jax.ShapeDty...  12.7 us
    all_to_all x1, blocking collectives, local(): parts = lax.all_to_all(parts, 'x', 0, 0, tiled=False)  11.8 us
    all_gather x1, blocking collectives, local(): pair = lax.all_gather(pair, 'y', axis=0, tiled=True)  10.9 us
    all_to_all x1, starting transfers between devices, local(): shared = lax.all_to_all(shared, mp, 0, 0, tiled=False).reshape(PAD, LANES)  8.28 us
    unnamed x42, local copies, waits for them, and re-layouts  8.1 us
  transfers between devices with their start and end apart: 9, of which 4 were waited for; matrix products, arithmetic and copies ran while one was open for 9% of the time, Pallas kernels for 1%

profile of v4, /device:TPU:1, one launch (start us, length us, event | category | flops | bytes accessed | tf_op | source)
XLA Modules:
  0.0 213.0 jit_solution(6305152246925103379)
XLA Ops:
  11.7 10.9 %all_gather.12 = bf16[256,640]{1,0:T(8,128)(2,1)S(1)} all-gather(bf16[64,640]{1,0:T(8,128)(2,1)S(1)} %shard_map.241), channel_id=1, replica_groups=mesh['z'=16,'y'=4,'x'=4,'c'=2] {'y'}, dimensions={0}, use_global_device_ids=true | all-gather | bytes 409600 | tf_op jit(solution)/shard_map/all_gather | solution.py:376
  24.3 40.5 %all-gather = bf16[1024,384]{1,0:T(8,128)(2,1)} all-gather(bf16[64,384]{1,0:T(8,128)(2,1)S(1)} %maximum_maximum_fusion), channel_id=2, replica_groups=mesh['z'=16,'y'=4,'x'=4,'c'=2] {'z'}, dimensions={0}, use_global_device_ids=true | all-gather | bytes 835584 | tf_op jit(solution)/shard_map/all_gather | solution.py:386
  64.8 3.4 %collective-permute-start.1 = (bf16[16,64,384]{2,1,0:T(8,128)(2,1)}, bf16[16,64,384]{2,1,0:T(8,128)(2,1)}, u32[]{:S(2)}, u32[]{:S(2)}) collective-permute-start(bf16[16,64,384]{2,1,0:T(8,128)(2,1)} %bitcast.3.own_hbm), channel_id=1, source_target_pairs={{0,24},{8,0},{16,8},{24,16},{1,25},{9,1},{17,9},{25,17},{2,26},{10... | collective-permute-start | bytes 2359304 | tf_op jit(solution)/shard_map/ppermute | solution.py:391
  68.2 1.9 collective-permute-start
  74.6 7.2 %all-to-all-start = ((f32[64,8,128]{2,1,0:T(8,128)}), f32[64,8,128]{2,1,0:T(8,128)S(1)}, u32[]{:S(2)}, u32[]{:S(2)}) async-start(f32[64,8,128]{2,1,0:T(8,128)} %shard_map.242), calls=%async_computation | async-start | bytes 524288 | tf_op jit(solution)/shard_map/all_to_all | solution.py:407
  81.8 2.7 %fusion = f32[384]{0:T(512)S(1)} fusion(bf16[1,384,4096]{2,1,0:T(8,128)(2,1)} %param.18), kind=kLoop, calls=%fused_computation.2 | loop fusion | flops 4718208 | bytes 3147264 | tf_op jit(solution)/shard_map/reduce_sum | solution.py:415
  86.8 1.8 slice.46
  88.6 4.1 %collective-permute-start.3 = (bf16[8,64,384]{2,1,0:T(8,128)(2,1)}, bf16[8,64,384]{2,1,0:T(8,128)(2,1)}, u32[]{:S(2)}, u32[]{:S(2)}) collective-permute-start(bf16[8,64,384]{2,1,0:T(8,128)(2,1)} %slice.46), channel_id=1, source_target_pairs={{0,24},{8,0},{16,8},{24,16},{1,25},{9,1},{17,9},{25,17},{2,26},{10... | collective-permute-start | bytes 1179656 | tf_op jit(solution)/shard_map/ppermute | solution.py:393
  92.7 1.8 slice.45
  94.5 1.9 collective-permute-start.2
  96.5 1.4 slice_bitcast_fusion.1
  97.9 1.7 slice_bitcast_fusion
  99.6 1.8 all-to-all-done
  102.1 1.3 broadcast_in_dim.7
  103.4 18.0 %all-to-all-start.1 = ((f32[8,8,128]{2,1,0:T(8,128)}), f32[8,8,128]{2,1,0:T(8,128)}, u32[]{:S(2)}, u32[]{:S(2)}) async-start(f32[8,8,128]{2,1,0:T(8,128)} %broadcast_in_dim.7), calls=%async_computation.1 | async-start | bytes 65536 | tf_op jit(solution)/shard_map/all_to_all | solution.py:408
  124.3 1.9 all-to-all-done.1.cols_ref
  126.2 2.2 %copy-done = bf16[4096,512]{1,0:T(8,128)(2,1)S(1)} copy-done((bf16[4096,512]{1,0:T(8,128)(2,1)S(1)}, bf16[4096,512]{1,0:T(8,128)(2,1)}, u32[]{:S(2)}) %copy-start) | copy-done | bytes 4194328
  129.8 12.7 %shard_map.243 = (f32[4,16,4224]{2,1,0:T(8,128)S(1)}, f32[4,16,4224]{2,1,0:T(8,128)S(1)}, f32[16,4096]{1,0:T(8,128)S(1)}, f32[16,4096]{1,0:T(8,128)S(1)}, f32[16,128]{1,0:T(8,128)S(1)}, /*index=5*/f32[1,4096]{1,0:T(1,128)S(1)}) custom-call(s32[6]{0:T(128)S(1)} %copy-done.16, bf16[4096,512]{1,0:T(8,128)(2,1)S(1)} %copy-done, ...), custom_call_target="tpu_custom_call" | custom-call | tf_op jit(solution)/shard_map/pallas_call | solution.py:250
  142.5 2.8 %collective-permute-start.4 = (f32[4,16,4224]{2,1,0:T(8,128)S(1)}, f32[4,16,4224]{2,1,0:T(8,128)S(1)}, u32[]{:S(2)}, u32[]{:S(2)}) collective-permute-start(f32[4,16,4224]{2,1,0:T(8,128)S(1)} %get-tuple-element.28), channel_id=1, source_target_pairs={{0,1},{1,0},{2,3},{3,2},{4,5},{5,4},{6,7},{7,6},{8,9},{9,8},{10,11... | collective-permute-start | bytes 3244040 | tf_op jit(solution)/shard_map/ppermute | solution.py:435
  145.3 2.3 %collective-permute-done.4 = f32[4,16,4224]{2,1,0:T(8,128)S(1)} collective-permute-done((f32[4,16,4224]{2,1,0:T(8,128)S(1)}, f32[4,16,4224]{2,1,0:T(8,128)S(1)}, u32[]{:S(2)}, u32[]{:S(2)}) %collective-permute-start.4) | collective-permute-done | bytes 1081376 | tf_op jit(solution)/shard_map/ppermute | solution.py:435
  147.8 11.8 %all_to_all.25.refs_0_ = bf16[4,16,4224]{2,1,0:T(8,128)(2,1)S(1)} all-to-all(bf16[4,16,4224]{2,1,0:T(8,128)(2,1)S(1)} %add_convert_fusion), channel_id=1, replica_groups=mesh['z'=16,'y'=4,'x'=4,'c'=2] {'x'}, dimensions={0} | all-to-all | bytes 1081344 | tf_op jit(solution)/shard_map/all_to_all | solution.py:436
  159.9 31.2 %all_to_all.26.back_ref = bf16[64,16,128]{2,1,0:T(8,128)(2,1)S(1)} all-to-all(bf16[64,16,128]{2,1,0:T(8,128)(2,1)S(1)} %shard_map.244), channel_id=1, replica_groups=mesh['z'=16,'y'=4,'x'=4,'c'=2] {'z','y'}, dimensions={0} | all-to-all | bytes 524288 | tf_op jit(solution)/shard_map/all_to_all | solution.py:445
  192.2 8.3 %all-to-all-start.4 = ((f32[8,16,128]{2,1,0:T(8,128)}), f32[8,16,128]{2,1,0:T(8,128)S(1)}, u32[]{:S(2)}, u32[]{:S(2)}) async-start(f32[8,16,128]{2,1,0:T(8,128)} %get-tuple-element.33), calls=%async_computation.4 | async-start | bytes 131072 | tf_op jit(solution)/shard_map/all_to_all | solution.py:456
  201.3 4.1 %all-to-all-done.4 = f32[8,16,128]{2,1,0:T(8,128)S(1)} async-done(((f32[8,16,128]{2,1,0:T(8,128)}), f32[8,16,128]{2,1,0:T(8,128)S(1)}, u32[]{:S(2)}, u32[]{:S(2)}) %all-to-all-start.4) | async-done | bytes 65568 | tf_op jit(solution)/shard_map/all_to_all | solution.py:456
  (71 shorter events, 20.3 us)
Async XLA Ops:
  7.2 119.1 %all-gather.3.cloned.1.call-start = ((), (), s32[]{:S(2)}) async-start(), calls=%async_computation.5 | async-start | bytes 4456448 | tf_op jit(solution)/shard_map/all_gather | solution.py:385
  11.7 72.9 %copy-start.3 = (f32[4096]{0:T(1024)S(1)}, f32[4096]{0:T(1024)}, u32[]{:S(2)}) copy-start(f32[4096]{0:T(1024)} %param.19) | copy-start | bytes 49156
  64.8 22.0 %collective-permute-start.1 = (bf16[16,64,384]{2,1,0:T(8,128)(2,1)}, bf16[16,64,384]{2,1,0:T(8,128)(2,1)}, u32[]{:S(2)}, u32[]{:S(2)}) collective-permute-start(bf16[16,64,384]{2,1,0:T(8,128)(2,1)} %bitcast.3.own_hbm), channel_id=1, source_target_pairs={{0,24},{8,0},{16,8},{24,16},{1,25},{9,1},{17,9},{25,17},{2,26},{10... | collective-permute-start | bytes 2359304 | tf_op jit(solution)/shard_map/ppermute | solution.py:391
  68.2 24.5 %collective-permute-start = (bf16[16,64,384]{2,1,0:T(8,128)(2,1)}, bf16[16,64,384]{2,1,0:T(8,128)(2,1)}, u32[]{:S(2)}, u32[]{:S(2)}) collective-permute-start(bf16[16,64,384]{2,1,0:T(8,128)(2,1)} %bitcast.3.own_hbm), channel_id=1, source_target_pairs={{0,8},{8,16},{16,24},{24,0},{1,9},{9,17},{17,25},{25,1},{2,10},{10... | collective-permute-start | bytes 2359304 | tf_op jit(solution)/shard_map/ppermute | solution.py:390
  71.7 0.9 copy-start.1
  72.7 0.8 copy-start.5
  74.6 26.9 %all-to-all-start = ((f32[64,8,128]{2,1,0:T(8,128)}), f32[64,8,128]{2,1,0:T(8,128)S(1)}, u32[]{:S(2)}, u32[]{:S(2)}) async-start(f32[64,8,128]{2,1,0:T(8,128)} %shard_map.242), calls=%async_computation | async-start | bytes 524288 | tf_op jit(solution)/shard_map/all_to_all | solution.py:407
  81.8 2.9 %copy-start.18 = (bf16[1,384,4096]{2,1,0:T(8,128)(2,1)S(1)}, bf16[1,384,4096]{2,1,0:T(8,128)(2,1)}, u32[]{:S(2)}) copy-start(bf16[1,384,4096]{2,1,0:T(8,128)(2,1)} %param.18) | copy-start | bytes 9437188
  88.6 37.6 %collective-permute-start.3 = (bf16[8,64,384]{2,1,0:T(8,128)(2,1)}, bf16[8,64,384]{2,1,0:T(8,128)(2,1)}, u32[]{:S(2)}, u32[]{:S(2)}) collective-permute-start(bf16[8,64,384]{2,1,0:T(8,128)(2,1)} %slice.46), channel_id=1, source_target_pairs={{0,24},{8,0},{16,8},{24,16},{1,25},{9,1},{17,9},{25,17},{2,26},{10... | collective-permute-start | bytes 1179656 | tf_op jit(solution)/shard_map/ppermute | solution.py:393
  94.5 31.7 %collective-permute-start.2 = (bf16[8,64,384]{2,1,0:T(8,128)(2,1)}, bf16[8,64,384]{2,1,0:T(8,128)(2,1)}, u32[]{:S(2)}, u32[]{:S(2)}) collective-permute-start(bf16[8,64,384]{2,1,0:T(8,128)(2,1)} %slice.45), channel_id=1, source_target_pairs={{0,8},{8,16},{16,24},{24,0},{1,9},{9,17},{17,25},{25,1},{2,10},{10... | collective-permute-start | bytes 1179656 | tf_op jit(solution)/shard_map/ppermute | solution.py:392
  103.4 22.8 %all-to-all-start.1 = ((f32[8,8,128]{2,1,0:T(8,128)}), f32[8,8,128]{2,1,0:T(8,128)}, u32[]{:S(2)}, u32[]{:S(2)}) async-start(f32[8,8,128]{2,1,0:T(8,128)} %broadcast_in_dim.7), calls=%async_computation.1 | async-start | bytes 65536 | tf_op jit(solution)/shard_map/all_to_all | solution.py:408
  126.2 2.2 %copy-start = (bf16[4096,512]{1,0:T(8,128)(2,1)S(1)}, bf16[4096,512]{1,0:T(8,128)(2,1)}, u32[]{:S(2)}) copy-start(bf16[4096,512]{1,0:T(8,128)(2,1)} %all-gather.3.cloned.1.call-done.pair_hbm) | copy-start | bytes 12582916
  142.5 48.7 %copy-start.15 = (s32[64]{0:T(128)S(1)}, s32[64]{0:T(128)}, u32[]{:S(2)}) copy-start(s32[64]{0:T(128)} %copy-done.14) | copy-start | bytes 772
  142.5 58.0 %copy-start.2 = (f32[64,512]{1,0:T(8,128)S(1)}, f32[64,512]{1,0:T(8,128)}, u32[]{:S(2)}) copy-start(f32[64,512]{1,0:T(8,128)} %col_ref.1) | copy-start | bytes 393220
  142.5 58.0 %copy-start.19 = (f32[64,512]{1,0:T(8,128)S(1)}, f32[64,512]{1,0:T(8,128)}, u32[]{:S(2)}) copy-start(f32[64,512]{1,0:T(8,128)} %param.32) | copy-start | bytes 393220
  142.5 58.0 %copy-start.20 = (f32[64,512]{1,0:T(8,128)S(1)}, f32[64,512]{1,0:T(8,128)}, u32[]{:S(2)}) copy-start(f32[64,512]{1,0:T(8,128)} %param.33) | copy-start | bytes 393220
  142.5 5.1 %collective-permute-start.4 = (f32[4,16,4224]{2,1,0:T(8,128)S(1)}, f32[4,16,4224]{2,1,0:T(8,128)S(1)}, u32[]{:S(2)}, u32[]{:S(2)}) collective-permute-start(f32[4,16,4224]{2,1,0:T(8,128)S(1)} %get-tuple-element.28), channel_id=1, source_target_pairs={{0,1},{1,0},{2,3},{3,2},{4,5},{5,4},{6,7},{7,6},{8,9},{9,8},{10,11... | collective-permute-start | bytes 3244040 | tf_op jit(solution)/shard_map/ppermute | solution.py:435
  147.6 57.7 %copy-start.4 = (f32[100,64]{0,1:T(8,128)S(1)}, f32[100,64]{0,1:T(8,128)}, u32[]{:S(2)}) copy-start(f32[100,64]{0,1:T(8,128)} %param.25) | copy-start | bytes 76804
  147.6 57.7 %copy-start.6 = (f32[64,100]{1,0:T(8,128)S(1)}, f32[64,100]{1,0:T(8,128)}, u32[]{:S(2)}) copy-start(f32[64,100]{1,0:T(8,128)} %refs_1_.3) | copy-start | bytes 76804
  147.6 57.7 %copy-start.9 = (f32[100,64]{0,1:T(8,128)S(1)}, f32[100,64]{0,1:T(8,128)}, u32[]{:S(2)}) copy-start(f32[100,64]{0,1:T(8,128)} %param.26) | copy-start | bytes 76804
  147.6 57.7 %copy-start.10 = (f32[64,100]{1,0:T(8,128)S(1)}, f32[64,100]{1,0:T(8,128)}, u32[]{:S(2)}) copy-start(f32[64,100]{1,0:T(8,128)} %refs_3_.3) | copy-start | bytes 76804
  147.6 57.7 %copy-start.11 = (f32[100,64]{0,1:T(8,128)S(1)}, f32[100,64]{0,1:T(8,128)}, u32[]{:S(2)}) copy-start(f32[100,64]{0,1:T(8,128)} %param.27) | copy-start | bytes 76804
  147.6 57.7 %copy-start.12 = (f32[64,100]{1,0:T(8,128)S(1)}, f32[64,100]{1,0:T(8,128)}, u32[]{:S(2)}) copy-start(f32[64,100]{1,0:T(8,128)} %refs_5_.1) | copy-start | bytes 76804
  192.2 13.1 %all-to-all-start.4 = ((f32[8,16,128]{2,1,0:T(8,128)}), f32[8,16,128]{2,1,0:T(8,128)S(1)}, u32[]{:S(2)}, u32[]{:S(2)}) async-start(f32[8,16,128]{2,1,0:T(8,128)} %get-tuple-element.33), calls=%async_computation.4 | async-start | bytes 131072 | tf_op jit(solution)/shard_map/all_to_all | solution.py:456
  (6 other events, 4.1 us)
Sparse Core Ops, SparseCore 0:
  24.4 89.6 all-gather.2

commit v5 on v4

--- a/solution.py
+++ b/solution.py
@@ -26,7 +26,8 @@
 VMEM = pl.BlockSpec(memory_space=pltpu.VMEM)
 SMEM = pl.BlockSpec(memory_space=pltpu.SMEM)
 PARAMS = pltpu.CompilerParams(vmem_limit_bytes=16 * 1024 * 1024)
-MAIN_PARAMS = pltpu.CompilerParams(vmem_limit_bytes=32 * 1024 * 1024)
+MAIN_PARAMS = pltpu.CompilerParams(vmem_limit_bytes=50 * 1024 * 1024)
+ALONE_PARAMS = pltpu.CompilerParams(vmem_limit_bytes=58 * 1024 * 1024)
 
 
 def adam_step(param, moment_one, moment_two, gradient):
@@ -257,7 +258,7 @@
             jax.ShapeDtypeStruct((BLOCK, LANES), F32),
             jax.ShapeDtypeStruct((1, width), F32),
         ),
-        in_specs=[SMEM, pl.BlockSpec(memory_space=pltpu.HBM)]
+        in_specs=[SMEM, pl.BlockSpec(memory_space=pl.ANY)]
         + [pl.BlockSpec(memory_space=pl.ANY)] * 5
         + [VMEM] * 6,
         out_specs=(VMEM,) * 6,
@@ -371,7 +372,7 @@
         out_shape=jax.ShapeDtypeStruct((depth, 2 * inner + LANES), BF16),
         in_specs=[SMEM, SMEM, VMEM, VMEM],
         out_specs=VMEM,
-        compiler_params=PARAMS,
+        compiler_params=ALONE_PARAMS,
     )(row_tenant, tenant_slot, w_key, w_value)
     pair = lax.all_gather(pair, "y", axis=0, tiled=True)
     marks = pair.reshape(ring, depth, -1)[:, 0, 2 * inner : 2 * inner + 2].reshape(-1)
@@ -402,7 +403,7 @@
         out_shape=jax.ShapeDtypeStruct((count, 8, LANES), F32),
         in_specs=[SMEM, VMEM, VMEM, VMEM],
         out_specs=VMEM,
-        compiler_params=PARAMS,
+        compiler_params=ALONE_PARAMS,
     )(first, slots, row_factor, col_factor)
     terms = jnp.sum(lax.all_to_all(terms, dp, 0, 0, tiled=False), axis=0)
     factor_cols = lax.all_to_all(

time: 215 us -> 206 us (0.958)
  local copies, waits for them, and re-layouts: 19.9 us -> 6.21 us
  waiting for transfers between devices: 10.2 us -> 14.7 us
  Pallas kernels: 16.8 us -> 20.5 us
  blocking collectives: 94.3 us -> 90.8 us
    unnamed x42 -> x26, local copies, waits for them, and re-layouts: 8.1 us -> 1.03 us
    all_to_all x1, waiting for transfers between devices: 1.92 us -> 4.57 us  [local(): lax.all_to_all(jnp.broadcast_to(terms[None], (groups, 8, LANES)), mp, 0,...]
  transfers between devices with their start and end apart: 9 -> 9, of which waited for: 4 -> 4; matrix products, arithmetic and copies ran while one was open for 9% -> 6% of each run, Pallas kernels for 1% -> 1%
where the time goes in v5:
time: 206 us; the launch traced here: 205 us
  blocking collectives  90.8 us (44%)
  starting transfers between devices  48 us (23%)
  Pallas kernels  20.5 us (10%)
  between operations  15 us (7%)
  waiting for transfers between devices  14.7 us (7%)
  other arithmetic  10.2 us (5%)
  local copies, waits for them, and re-layouts  6.21 us (3%)
    all_gather x1, blocking collectives, local(): own = lax.all_gather(own, 'z', axis=0, tiled=False)  38.4 us
    all_to_all x1, blocking collectives, local(): back = lax.all_to_all(outgoing, dp, 0, 0, tiled=False)  29.4 us
    all_to_all x1, starting transfers between devices, local(): lax.all_to_all(jnp.broadcast_to(terms[None], (groups, 8, LANES)), mp, 0,...  18.3 us
    pallas_call x1, Pallas kernels, main_part(): pl.pallas_call(main_kernel, out_shape=(half, half, own, own, jax.ShapeDty...  14.6 us
    all_to_all x1, blocking collectives, local(): parts = lax.all_to_all(parts, 'x', 0, 0, tiled=False)  11.8 us
    all_gather x1, blocking collectives, local(): pair = lax.all_gather(pair, 'y', axis=0, tiled=True)  11.2 us
    all_to_all x1, starting transfers between devices, local(): shared = lax.all_to_all(shared, mp, 0, 0, tiled=False).reshape(PAD, LANES)  8.31 us
    all_to_all x1, starting transfers between devices, local(): terms = jnp.sum(lax.all_to_all(terms, dp, 0, 0, tiled=False), axis=0)  7.27 us
  transfers between devices with their start and end apart: 9, of which 4 were waited for; matrix products, arithmetic and copies ran while one was open for 6% of the time, Pallas kernels for 1%

profile of v5, /device:TPU:1, one launch (start us, length us, event | category | flops | bytes accessed | tf_op | source)
XLA Modules:
  0.0 205.3 jit_solution(4882556119776660858)
XLA Ops:
  8.6 1.6 shard_map.241
  10.2 11.2 %all_gather.12 = bf16[256,640]{1,0:T(8,128)(2,1)S(1)} all-gather(bf16[64,640]{1,0:T(8,128)(2,1)} %shard_map.241), channel_id=1, replica_groups=mesh['z'=16,'y'=4,'x'=4,'c'=2] {'y'}, dimensions={0}, use_global_device_ids=true | all-gather | bytes 409600 | tf_op jit(solution)/shard_map/all_gather | solution.py:377
  23.1 38.4 %all-gather = bf16[1024,384]{1,0:T(8,128)(2,1)S(1)} all-gather(bf16[64,384]{1,0:T(8,128)(2,1)S(1)} %maximum_maximum_fusion), channel_id=2, replica_groups=mesh['z'=16,'y'=4,'x'=4,'c'=2] {'z'}, dimensions={0}, use_global_device_ids=true | all-gather | bytes 835584 | tf_op jit(solution)/shard_map/all_gather | solution.py:387
  61.5 1.9 collective-permute-start.1
  63.4 3.4 %collective-permute-start = (bf16[16,64,384]{2,1,0:T(8,128)(2,1)S(1)}, bf16[16,64,384]{2,1,0:T(8,128)(2,1)S(1)}, u32[]{:S(2)}, u32[]{:S(2)}) collective-permute-start(bf16[16,64,384]{2,1,0:T(8,128)(2,1)S(1)} %bitcast.29), channel_id=1, source_target_pairs={{0,8},{8,16},{16,24},{24,0},{1,9},{9,17},{17,25},{25,1},{2,10},{10... | collective-permute-start | bytes 2359304 | tf_op jit(solution)/shard_map/ppermute | solution.py:391
  67.7 2.1 %shard_map.242 = f32[64,8,128]{2,1,0:T(8,128)} custom-call(s32[1]{0:T(128)} %bitcast.first_ref, s32[1,64]{1,0:T(1,128)} %bitcast.38, f32[64,100]{1,0:T(8,128)} %refs_1_.3, f32[64,512]{1,0:T(8,128)} %col_ref.1), custom_call_target="tpu_custom_call" | custom-call | tf_op jit(solution)/shard_map/pallas_call | solution.py:401
  69.8 7.3 %all-to-all-start = ((f32[64,8,128]{2,1,0:T(8,128)}), f32[64,8,128]{2,1,0:T(8,128)S(1)}, u32[]{:S(2)}, u32[]{:S(2)}) async-start(f32[64,8,128]{2,1,0:T(8,128)} %shard_map.242), calls=%async_computation | async-start | bytes 524288 | tf_op jit(solution)/shard_map/all_to_all | solution.py:408
  77.0 2.8 %fusion = f32[384]{0:T(512)S(1)} fusion(bf16[1,384,4096]{2,1,0:T(8,128)(2,1)} %param.18), kind=kLoop, calls=%fused_computation.2 | loop fusion | flops 4718208 | bytes 3147264 | tf_op jit(solution)/shard_map/reduce_sum | solution.py:416
  79.9 2.7 %fusion.2.hidden_ref = bf16[384,4096]{1,0:T(8,128)(2,1)} fusion(bf16[1,384,4096]{2,1,0:T(8,128)(2,1)S(1)} %copy-done.8, f32[4096]{0:T(1024)S(1)} %copy-done, f32[384]{0:T(512)S(1)} %add_rsqrt_fusion), kind=kLoop, calls=%fused_computation.4 | loop fusion | flops 6291456 | bytes 6309376 | tf_op jit(solution)/shard_map/convert_element_type | solution.py:417
  84.5 4.1 %collective-permute-start.3 = (bf16[8,64,384]{2,1,0:T(8,128)(2,1)S(1)}, bf16[8,64,384]{2,1,0:T(8,128)(2,1)S(1)}, u32[]{:S(2)}, u32[]{:S(2)}) collective-permute-start(bf16[8,64,384]{2,1,0:T(8,128)(2,1)S(1)} %slice.46), channel_id=1, source_target_pairs={{0,24},{8,0},{16,8},{24,16},{1,25},{9,1},{17,9},{25,17},{2,26},{10... | collective-permute-start | bytes 1179656 | tf_op jit(solution)/shard_map/ppermute | solution.py:394
  89.5 1.9 collective-permute-start.2
  92.2 1.0 slice_bitcast_fusion
  93.2 3.5 %all-to-all-done = f32[64,8,128]{2,1,0:T(8,128)S(1)} async-done(((f32[64,8,128]{2,1,0:T(8,128)}), f32[64,8,128]{2,1,0:T(8,128)S(1)}, u32[]{:S(2)}, u32[]{:S(2)}) %all-to-all-start) | async-done | bytes 262176 | tf_op jit(solution)/shard_map/all_to_all | solution.py:408
  97.4 18.3 %all-to-all-start.1 = ((f32[8,8,128]{2,1,0:T(8,128)}), f32[8,8,128]{2,1,0:T(8,128)S(1)}, u32[]{:S(2)}, u32[]{:S(2)}) async-start(f32[8,8,128]{2,1,0:T(8,128)} %broadcast_in_dim.7), calls=%async_computation.1 | async-start | bytes 65536 | tf_op jit(solution)/shard_map/all_to_all | solution.py:409
  115.9 4.6 %all-to-all-done.1.cols_ref = f32[8,8,128]{2,1,0:T(8,128)S(1)} async-done(((f32[8,8,128]{2,1,0:T(8,128)}), f32[8,8,128]{2,1,0:T(8,128)S(1)}, u32[]{:S(2)}, u32[]{:S(2)}) %all-to-all-start.1) | async-done | bytes 32800 | tf_op jit(solution)/shard_map/all_to_all | solution.py:409
  120.5 14.6 %shard_map.243 = (f32[4,16,4224]{2,1,0:T(8,128)}, f32[4,16,4224]{2,1,0:T(8,128)}, f32[16,4096]{1,0:T(8,128)S(1)}, f32[16,4096]{1,0:T(8,128)S(1)}, f32[16,128]{1,0:T(8,128)S(1)}, /*index=5*/f32[1,4096]{1,0:T(1,128)S(1)}) custom-call(s32[6]{0:T(128)S(1)} %stack.27.place_ref, bf16[4096,512]{1,0:T(8,128)(2,1)} %all-gather.3.cloned.1.call-done.pair_hbm, ...), custom_call_target="tpu_custom_call" | custom-call | tf_op jit(solution)/shard_map/pallas_call | solution.py:251
  135.1 2.8 %collective-permute-start.4 = (f32[4,16,4224]{2,1,0:T(8,128)}, f32[4,16,4224]{2,1,0:T(8,128)S(1)}, u32[]{:S(2)}, u32[]{:S(2)}) collective-permute-start(f32[4,16,4224]{2,1,0:T(8,128)} %get-tuple-element.28), channel_id=1, source_target_pairs={{0,1},{1,0},{2,3},{3,2},{4,5},{5,4},{6,7},{7,6},{8,9},{9,8},{10,11... | collective-permute-start | bytes 3244040 | tf_op jit(solution)/shard_map/ppermute | solution.py:436
  137.9 2.5 %collective-permute-done.4 = f32[4,16,4224]{2,1,0:T(8,128)S(1)} collective-permute-done((f32[4,16,4224]{2,1,0:T(8,128)}, f32[4,16,4224]{2,1,0:T(8,128)S(1)}, u32[]{:S(2)}, u32[]{:S(2)}) %collective-permute-start.4) | collective-permute-done | bytes 1081376 | tf_op jit(solution)/shard_map/ppermute | solution.py:436
  140.4 1.4 add_convert_fusion
  141.9 11.8 %all_to_all.25.refs_0_ = bf16[4,16,4224]{2,1,0:T(8,128)(2,1)S(1)} all-to-all(bf16[4,16,4224]{2,1,0:T(8,128)(2,1)S(1)} %add_convert_fusion), channel_id=1, replica_groups=mesh['z'=16,'y'=4,'x'=4,'c'=2] {'x'}, dimensions={0} | all-to-all | bytes 1081344 | tf_op jit(solution)/shard_map/all_to_all | solution.py:437
  154.0 29.4 %all_to_all.26.back_ref = bf16[64,16,128]{2,1,0:T(8,128)(2,1)S(1)} all-to-all(bf16[64,16,128]{2,1,0:T(8,128)(2,1)S(1)} %shard_map.244), channel_id=1, replica_groups=mesh['z'=16,'y'=4,'x'=4,'c'=2] {'z','y'}, dimensions={0} | all-to-all | bytes 524288 | tf_op jit(solution)/shard_map/all_to_all | solution.py:446
  183.4 1.0 shard_map.245
  184.5 8.3 %all-to-all-start.4 = ((f32[8,16,128]{2,1,0:T(8,128)}), f32[8,16,128]{2,1,0:T(8,128)S(1)}, u32[]{:S(2)}, u32[]{:S(2)}) async-start(f32[8,16,128]{2,1,0:T(8,128)} %get-tuple-element.33), calls=%async_computation.4 | async-start | bytes 131072 | tf_op jit(solution)/shard_map/all_to_all | solution.py:457
  193.6 4.1 %all-to-all-done.4 = f32[8,16,128]{2,1,0:T(8,128)S(1)} async-done(((f32[8,16,128]{2,1,0:T(8,128)}), f32[8,16,128]{2,1,0:T(8,128)S(1)}, u32[]{:S(2)}, u32[]{:S(2)}) %all-to-all-start.4) | async-done | bytes 65568 | tf_op jit(solution)/shard_map/all_to_all | solution.py:457
  (55 shorter events, 9.7 us)
Async XLA Ops:
  7.2 113.3 %all-gather.3.cloned.1.call-start = ((), (), s32[]{:S(2)}) async-start(), calls=%async_computation.5 | async-start | bytes 4456448 | tf_op jit(solution)/shard_map/all_gather | solution.py:386
  10.2 69.6 %copy-start = (f32[4096]{0:T(1024)S(1)}, f32[4096]{0:T(1024)}, u32[]{:S(2)}) copy-start(f32[4096]{0:T(1024)} %param.19) | copy-start | bytes 49156
  61.5 22.1 %collective-permute-start.1 = (bf16[16,64,384]{2,1,0:T(8,128)(2,1)S(1)}, bf16[16,64,384]{2,1,0:T(8,128)(2,1)S(1)}, u32[]{:S(2)}, u32[]{:S(2)}) collective-permute-start(bf16[16,64,384]{2,1,0:T(8,128)(2,1)S(1)} %bitcast.28), channel_id=1, source_target_pairs={{0,24},{8,0},{16,8},{24,16},{1,25},{9,1},{17,9},{25,17},{2,26},{10... | collective-permute-start | bytes 2359304 | tf_op jit(solution)/shard_map/ppermute | solution.py:392
  63.4 25.3 %collective-permute-start = (bf16[16,64,384]{2,1,0:T(8,128)(2,1)S(1)}, bf16[16,64,384]{2,1,0:T(8,128)(2,1)S(1)}, u32[]{:S(2)}, u32[]{:S(2)}) collective-permute-start(bf16[16,64,384]{2,1,0:T(8,128)(2,1)S(1)} %bitcast.29), channel_id=1, source_target_pairs={{0,8},{8,16},{16,24},{24,0},{1,9},{9,17},{17,25},{25,1},{2,10},{10... | collective-permute-start | bytes 2359304 | tf_op jit(solution)/shard_map/ppermute | solution.py:391
  69.8 26.9 %all-to-all-start = ((f32[64,8,128]{2,1,0:T(8,128)}), f32[64,8,128]{2,1,0:T(8,128)S(1)}, u32[]{:S(2)}, u32[]{:S(2)}) async-start(f32[64,8,128]{2,1,0:T(8,128)} %shard_map.242), calls=%async_computation | async-start | bytes 524288 | tf_op jit(solution)/shard_map/all_to_all | solution.py:408
  77.0 2.9 %copy-start.8 = (bf16[1,384,4096]{2,1,0:T(8,128)(2,1)S(1)}, bf16[1,384,4096]{2,1,0:T(8,128)(2,1)}, u32[]{:S(2)}) copy-start(bf16[1,384,4096]{2,1,0:T(8,128)(2,1)} %param.18) | copy-start | bytes 9437188
  83.6 0.9 copy-start.9
  84.5 35.9 %collective-permute-start.3 = (bf16[8,64,384]{2,1,0:T(8,128)(2,1)S(1)}, bf16[8,64,384]{2,1,0:T(8,128)(2,1)S(1)}, u32[]{:S(2)}, u32[]{:S(2)}) collective-permute-start(bf16[8,64,384]{2,1,0:T(8,128)(2,1)S(1)} %slice.46), channel_id=1, source_target_pairs={{0,24},{8,0},{16,8},{24,16},{1,25},{9,1},{17,9},{25,17},{2,26},{10... | collective-permute-start | bytes 1179656 | tf_op jit(solution)/shard_map/ppermute | solution.py:394
  89.5 31.0 %collective-permute-start.2 = (bf16[8,64,384]{2,1,0:T(8,128)(2,1)}, bf16[8,64,384]{2,1,0:T(8,128)(2,1)S(1)}, u32[]{:S(2)}, u32[]{:S(2)}) collective-permute-start(bf16[8,64,384]{2,1,0:T(8,128)(2,1)} %slice.45), channel_id=1, source_target_pairs={{0,8},{8,16},{16,24},{24,0},{1,9},{9,17},{17,25},{25,1},{2,10},{10... | collective-permute-start | bytes 1179656 | tf_op jit(solution)/shard_map/ppermute | solution.py:393
  97.4 23.1 %all-to-all-start.1 = ((f32[8,8,128]{2,1,0:T(8,128)}), f32[8,8,128]{2,1,0:T(8,128)S(1)}, u32[]{:S(2)}, u32[]{:S(2)}) async-start(f32[8,8,128]{2,1,0:T(8,128)} %broadcast_in_dim.7), calls=%async_computation.1 | async-start | bytes 65536 | tf_op jit(solution)/shard_map/all_to_all | solution.py:409
  135.1 48.4 %copy-start.7 = (s32[64]{0:T(128)S(1)}, s32[64]{0:T(128)}, u32[]{:S(2)}) copy-start(s32[64]{0:T(128)} %fusion.6) | copy-start | bytes 772
  135.1 57.7 %copy-start.10 = (f32[64,512]{1,0:T(8,128)S(1)}, f32[64,512]{1,0:T(8,128)}, u32[]{:S(2)}) copy-start(f32[64,512]{1,0:T(8,128)} %col_ref.1) | copy-start | bytes 393220
  135.1 57.7 %copy-start.11 = (f32[64,512]{1,0:T(8,128)S(1)}, f32[64,512]{1,0:T(8,128)}, u32[]{:S(2)}) copy-start(f32[64,512]{1,0:T(8,128)} %param.32) | copy-start | bytes 393220
  135.1 57.7 %copy-start.12 = (f32[64,512]{1,0:T(8,128)S(1)}, f32[64,512]{1,0:T(8,128)}, u32[]{:S(2)}) copy-start(f32[64,512]{1,0:T(8,128)} %param.33) | copy-start | bytes 393220
  135.1 5.3 %collective-permute-start.4 = (f32[4,16,4224]{2,1,0:T(8,128)}, f32[4,16,4224]{2,1,0:T(8,128)S(1)}, u32[]{:S(2)}, u32[]{:S(2)}) collective-permute-start(f32[4,16,4224]{2,1,0:T(8,128)} %get-tuple-element.28), channel_id=1, source_target_pairs={{0,1},{1,0},{2,3},{3,2},{4,5},{5,4},{6,7},{7,6},{8,9},{9,8},{10,11... | collective-permute-start | bytes 3244040 | tf_op jit(solution)/shard_map/ppermute | solution.py:436
  140.4 57.2 %copy-start.1 = (f32[100,64]{0,1:T(8,128)S(1)}, f32[100,64]{0,1:T(8,128)}, u32[]{:S(2)}) copy-start(f32[100,64]{0,1:T(8,128)} %param.25) | copy-start | bytes 76804
  140.4 57.2 %copy-start.2 = (f32[64,100]{1,0:T(8,128)S(1)}, f32[64,100]{1,0:T(8,128)}, u32[]{:S(2)}) copy-start(f32[64,100]{1,0:T(8,128)} %refs_1_.3) | copy-start | bytes 76804
  140.4 57.2 %copy-start.3 = (f32[100,64]{0,1:T(8,128)S(1)}, f32[100,64]{0,1:T(8,128)}, u32[]{:S(2)}) copy-start(f32[100,64]{0,1:T(8,128)} %param.26) | copy-start | bytes 76804
  140.4 57.3 %copy-start.4 = (f32[64,100]{1,0:T(8,128)S(1)}, f32[64,100]{1,0:T(8,128)}, u32[]{:S(2)}) copy-start(f32[64,100]{1,0:T(8,128)} %refs_3_.3) | copy-start | bytes 76804
  140.4 57.3 %copy-start.5 = (f32[100,64]{0,1:T(8,128)S(1)}, f32[100,64]{0,1:T(8,128)}, u32[]{:S(2)}) copy-start(f32[100,64]{0,1:T(8,128)} %param.27) | copy-start | bytes 76804
  140.4 57.3 %copy-start.6 = (f32[64,100]{1,0:T(8,128)S(1)}, f32[64,100]{1,0:T(8,128)}, u32[]{:S(2)}) copy-start(f32[64,100]{1,0:T(8,128)} %refs_5_.1) | copy-start | bytes 76804
  184.5 13.2 %all-to-all-start.4 = ((f32[8,16,128]{2,1,0:T(8,128)}), f32[8,16,128]{2,1,0:T(8,128)S(1)}, u32[]{:S(2)}, u32[]{:S(2)}) async-start(f32[8,16,128]{2,1,0:T(8,128)} %get-tuple-element.33), calls=%async_computation.4 | async-start | bytes 131072 | tf_op jit(solution)/shard_map/all_to_all | solution.py:457
Sparse Core Ops, SparseCore 0:
  23.2 88.6 all-gather.2

commit v6 on v5

--- a/solution.py
+++ b/solution.py
@@ -237,7 +237,7 @@
         start = pl.multiple_of((2 * pair + core) * BLOCK, BLOCK)
         keep_ref[pair, :, :] = parts[pl.ds(start, BLOCK), :]
         start = pl.multiple_of((2 * pair + 1 - core) * BLOCK, BLOCK)
-        send_ref[pair, :, :] = parts[pl.ds(start, BLOCK), :]
+        send_ref[pair, :, :] = parts[pl.ds(start, BLOCK), :].astype(BF16)
 
 
 def main_part(place, pair, singles, hidden, up, cols, rows, gain, cot):
@@ -246,13 +246,13 @@
     inner = up.shape[1]
     ring = width // (singles[0].shape[0] * singles[0].shape[1])
     groups = cols.shape[0]
-    half = jax.ShapeDtypeStruct((groups // 2, BLOCK, width + LANES), F32)
+    half = (groups // 2, BLOCK, width + LANES)
     own = jax.ShapeDtypeStruct((BLOCK, width), F32)
     return pl.pallas_call(
         main_kernel,
         out_shape=(
-            half,
-            half,
+            jax.ShapeDtypeStruct(half, F32),
+            jax.ShapeDtypeStruct(half, BF16),
             own,
             own,
             jax.ShapeDtypeStruct((BLOCK, LANES), F32),
@@ -385,15 +385,6 @@
     pair, own = lax.optimization_barrier((pair, own))
     pair = lax.all_gather(pair, "z", axis=0, tiled=True)
     own = lax.all_gather(own, "z", axis=0, tiled=False)
-    half = own.shape[0] // 2
-    up_ring = [(i, (i + 1) % ring) for i in range(ring)]
-    down_ring = [(i, (i - 1) % ring) for i in range(ring)]
-    left = lax.ppermute(own, "y", up_ring)
-    right = lax.ppermute(own, "y", down_ring)
-    far_first = lax.ppermute(left[:half], "y", up_ring)
-    far_second = lax.ppermute(right[half:], "y", down_ring)
-    singles = (own, left, right, far_first, far_second)
-
     marks = own[:, 0, inner + PROMPT : inner + PROMPT + 2 * ring].reshape(count, 2)
     marks = marks.astype(jnp.int32)
     slots = (marks[:, 0] * owned + marks[:, 1])[None, :]
@@ -405,7 +396,16 @@
         out_specs=VMEM,
         compiler_params=ALONE_PARAMS,
     )(first, slots, row_factor, col_factor)
+    own, terms = lax.optimization_barrier((own, terms))
     terms = jnp.sum(lax.all_to_all(terms, dp, 0, 0, tiled=False), axis=0)
+    half = own.shape[0] // 2
+    up_ring = [(i, (i + 1) % ring) for i in range(ring)]
+    down_ring = [(i, (i - 1) % ring) for i in range(ring)]
+    left = lax.ppermute(own, "y", up_ring)
+    right = lax.ppermute(own, "y", down_ring)
+    far_first = lax.ppermute(left[:half], "y", up_ring)
+    far_second = lax.ppermute(right[half:], "y", down_ring)
+    singles = (own, left, right, far_first, far_second)
     factor_cols = lax.all_to_all(
         jnp.broadcast_to(terms[None], (groups, 8, LANES)), mp, 0, 0, tiled=False
     )
@@ -433,7 +433,8 @@
         place, pair, singles, hidden, upstream, factor_cols, factor_rows, gain, cot
     )
 
-    parts = (keep + lax.ppermute(send, "c", [(0, 1), (1, 0)])).astype(BF16)
+    other = lax.ppermute(send, "c", [(0, 1), (1, 0)])
+    parts = (keep + other.astype(F32)).astype(BF16)
     parts = lax.all_to_all(parts, "x", 0, 0, tiled=False)
     outgoing = pl.pallas_call(
         lambda *refs: prompt_kernel(pieces, *refs),

time: 206 us -> 205 us (level)
  no operation moved by 1% of the time
where the time goes in v6:
time: 205 us; the launch traced here: 204 us
  blocking collectives  90.8 us (44%)
  starting transfers between devices  48.1 us (23%)
  Pallas kernels  20.1 us (10%)
  between operations  15 us (7%)
  waiting for transfers between devices  13.6 us (7%)
  other arithmetic  10.1 us (5%)
  local copies, waits for them, and re-layouts  6.31 us (3%)
    all_gather x1, blocking collectives, local(): own = lax.all_gather(own, 'z', axis=0, tiled=False)  38.4 us
    all_to_all x1, blocking collectives, local(): back = lax.all_to_all(outgoing, dp, 0, 0, tiled=False)  29.5 us
    all_to_all x1, starting transfers between devices, local(): lax.all_to_all(jnp.broadcast_to(terms[None], (groups, 8, LANES)), mp, 0,...  18.4 us
    pallas_call x1, Pallas kernels, main_part(): pl.pallas_call(main_kernel, out_shape=(jax.ShapeDtypeStruct(half, F32), j...  14.3 us
    all_to_all x1, blocking collectives, local(): parts = lax.all_to_all(parts, 'x', 0, 0, tiled=False)  11.8 us
    all_gather x1, blocking collectives, local(): pair = lax.all_gather(pair, 'y', axis=0, tiled=True)  11.2 us
    all_to_all x1, starting transfers between devices, local(): shared = lax.all_to_all(shared, mp, 0, 0, tiled=False).reshape(PAD, LANES)  8.31 us
    all_to_all x1, starting transfers between devices, local(): terms = jnp.sum(lax.all_to_all(terms, dp, 0, 0, tiled=False), axis=0)  7.28 us
  transfers between devices with their start and end apart: 9, of which 4 were waited for; matrix products, arithmetic and copies ran while one was open for 6% of the time, Pallas kernels for 1%

profile of v6, /device:TPU:1, one launch (start us, length us, event | category | flops | bytes accessed | tf_op | source)
XLA Modules:
  0.0 204.1 jit_solution(12587976928164643490)
XLA Ops:
  8.6 1.6 shard_map.241
  10.2 11.2 %all_gather.12 = bf16[256,640]{1,0:T(8,128)(2,1)S(1)} all-gather(bf16[64,640]{1,0:T(8,128)(2,1)} %shard_map.241), channel_id=1, replica_groups=mesh['z'=16,'y'=4,'x'=4,'c'=2] {'y'}, dimensions={0}, use_global_device_ids=true | all-gather | bytes 409600 | tf_op jit(solution)/shard_map/all_gather | solution.py:377
  23.1 38.4 %all-gather = bf16[1024,384]{1,0:T(8,128)(2,1)S(1)} all-gather(bf16[64,384]{1,0:T(8,128)(2,1)S(1)} %maximum_maximum_fusion), channel_id=2, replica_groups=mesh['z'=16,'y'=4,'x'=4,'c'=2] {'z'}, dimensions={0}, use_global_device_ids=true | all-gather | bytes 835584 | tf_op jit(solution)/shard_map/all_gather | solution.py:387
  62.4 2.1 %shard_map.242 = f32[64,8,128]{2,1,0:T(8,128)} custom-call(s32[1]{0:T(128)} %bitcast.first_ref, s32[1,64]{1,0:T(1,128)} %bitcast.38, f32[64,100]{1,0:T(8,128)} %refs_1_.3, f32[64,512]{1,0:T(8,128)} %col_ref.1), custom_call_target="tpu_custom_call" | custom-call | tf_op jit(solution)/shard_map/pallas_call | solution.py:392
  64.5 1.9 collective-permute-start.1
  66.4 3.4 %collective-permute-start = (bf16[16,64,384]{2,1,0:T(8,128)(2,1)S(1)}, bf16[16,64,384]{2,1,0:T(8,128)(2,1)S(1)}, u32[]{:S(2)}, u32[]{:S(2)}) collective-permute-start(bf16[16,64,384]{2,1,0:T(8,128)(2,1)S(1)} %bitcast.30), channel_id=1, source_target_pairs={{0,8},{8,16},{16,24},{24,0},{1,9},{9,17},{17,25},{25,1},{2,10},{10... | collective-permute-start | bytes 2359304 | tf_op jit(solution)/shard_map/ppermute | solution.py:404
  69.7 7.3 %all-to-all-start = ((f32[64,8,128]{2,1,0:T(8,128)}), f32[64,8,128]{2,1,0:T(8,128)S(1)}, u32[]{:S(2)}, u32[]{:S(2)}) async-start(f32[64,8,128]{2,1,0:T(8,128)} %shard_map.242), calls=%async_computation | async-start | bytes 524288 | tf_op jit(solution)/shard_map/all_to_all | solution.py:400
  77.1 2.8 %fusion = f32[384]{0:T(512)S(1)} fusion(bf16[1,384,4096]{2,1,0:T(8,128)(2,1)} %param.18), kind=kLoop, calls=%fused_computation.2 | loop fusion | flops 4718208 | bytes 3147264 | tf_op jit(solution)/shard_map/reduce_sum | solution.py:416
  79.9 2.7 %fusion.2.hidden_ref = bf16[384,4096]{1,0:T(8,128)(2,1)} fusion(bf16[1,384,4096]{2,1,0:T(8,128)(2,1)S(1)} %copy-done.8, f32[4096]{0:T(1024)S(1)} %copy-done, f32[384]{0:T(512)S(1)} %add_rsqrt_fusion), kind=kLoop, calls=%fused_computation.4 | loop fusion | flops 6291456 | bytes 6309376 | tf_op jit(solution)/shard_map/convert_element_type | solution.py:417
  84.6 4.1 %collective-permute-start.3 = (bf16[8,64,384]{2,1,0:T(8,128)(2,1)S(1)}, bf16[8,64,384]{2,1,0:T(8,128)(2,1)S(1)}, u32[]{:S(2)}, u32[]{:S(2)}) collective-permute-start(bf16[8,64,384]{2,1,0:T(8,128)(2,1)S(1)} %slice.46), channel_id=1, source_target_pairs={{0,24},{8,0},{16,8},{24,16},{1,25},{9,1},{17,9},{25,17},{2,26},{10... | collective-permute-start | bytes 1179656 | tf_op jit(solution)/shard_map/ppermute | solution.py:407
  89.6 1.9 collective-permute-start.2
  92.3 1.0 slice_bitcast_fusion
  93.3 3.4 %all-to-all-done = f32[64,8,128]{2,1,0:T(8,128)S(1)} async-done(((f32[64,8,128]{2,1,0:T(8,128)}), f32[64,8,128]{2,1,0:T(8,128)S(1)}, u32[]{:S(2)}, u32[]{:S(2)}) %all-to-all-start) | async-done | bytes 262176 | tf_op jit(solution)/shard_map/all_to_all | solution.py:400
  97.4 18.4 %all-to-all-start.1 = ((f32[8,8,128]{2,1,0:T(8,128)}), f32[8,8,128]{2,1,0:T(8,128)S(1)}, u32[]{:S(2)}, u32[]{:S(2)}) async-start(f32[8,8,128]{2,1,0:T(8,128)} %broadcast_in_dim.7), calls=%async_computation.1 | async-start | bytes 65536 | tf_op jit(solution)/shard_map/all_to_all | solution.py:409
  115.9 4.6 %all-to-all-done.1.cols_ref = f32[8,8,128]{2,1,0:T(8,128)S(1)} async-done(((f32[8,8,128]{2,1,0:T(8,128)}), f32[8,8,128]{2,1,0:T(8,128)S(1)}, u32[]{:S(2)}, u32[]{:S(2)}) %all-to-all-start.1) | async-done | bytes 32800 | tf_op jit(solution)/shard_map/all_to_all | solution.py:409
  120.5 14.3 %shard_map.243 = (f32[4,16,4224]{2,1,0:T(8,128)}, bf16[4,16,4224]{2,1,0:T(8,128)(2,1)S(1)}, f32[16,4096]{1,0:T(8,128)S(1)}, f32[16,4096]{1,0:T(8,128)S(1)}, f32[...) custom-call(s32[6]{0:T(128)S(1)} %stack.27.place_ref, bf16[4096,512]{1,0:T(8,128)(2,1)} %all-gather.3.cloned.1.call-done.pair_hbm, ...), custom_call_target="tpu_custom_call" | custom-call | tf_op jit(solution)/shard_map/pallas_call | solution.py:251
  134.8 2.8 %collective-permute-start.4 = (bf16[4,16,4224]{2,1,0:T(8,128)(2,1)S(1)}, bf16[4,16,4224]{2,1,0:T(8,128)(2,1)S(1)}, u32[]{:S(2)}, u32[]{:S(2)}) collective-permute-start(bf16[4,16,4224]{2,1,0:T(8,128)(2,1)S(1)} %get-tuple-element.32), channel_id=1, source_target_pairs={{0,1},{1,0},{2,3},{3,2},{4,5},{5,4},{6,7},{7,6},{8,9},{9,8},{10,11... | collective-permute-start | bytes 1622024 | tf_op jit(solution)/shard_map/ppermute | solution.py:436
  137.6 1.5 collective-permute-done.4
  139.2 1.4 add_convert_fusion
  140.5 11.8 %all_to_all.25.refs_0_ = bf16[4,16,4224]{2,1,0:T(8,128)(2,1)S(1)} all-to-all(bf16[4,16,4224]{2,1,0:T(8,128)(2,1)S(1)} %add_convert_fusion), channel_id=1, replica_groups=mesh['z'=16,'y'=4,'x'=4,'c'=2] {'x'}, dimensions={0} | all-to-all | bytes 1081344 | tf_op jit(solution)/shard_map/all_to_all | solution.py:438
  152.7 29.5 %all_to_all.26.back_ref = bf16[64,16,128]{2,1,0:T(8,128)(2,1)S(1)} all-to-all(bf16[64,16,128]{2,1,0:T(8,128)(2,1)S(1)} %shard_map.244), channel_id=1, replica_groups=mesh['z'=16,'y'=4,'x'=4,'c'=2] {'z','y'}, dimensions={0} | all-to-all | bytes 524288 | tf_op jit(solution)/shard_map/all_to_all | solution.py:447
  182.2 1.0 shard_map.245
  183.2 8.3 %all-to-all-start.4 = ((f32[8,16,128]{2,1,0:T(8,128)}), f32[8,16,128]{2,1,0:T(8,128)S(1)}, u32[]{:S(2)}, u32[]{:S(2)}) async-start(f32[8,16,128]{2,1,0:T(8,128)} %get-tuple-element.37), calls=%async_computation.4 | async-start | bytes 131072 | tf_op jit(solution)/shard_map/all_to_all | solution.py:458
  192.3 4.1 %all-to-all-done.4 = f32[8,16,128]{2,1,0:T(8,128)S(1)} async-done(((f32[8,16,128]{2,1,0:T(8,128)}), f32[8,16,128]{2,1,0:T(8,128)S(1)}, u32[]{:S(2)}, u32[]{:S(2)}) %all-to-all-start.4) | async-done | bytes 65568 | tf_op jit(solution)/shard_map/all_to_all | solution.py:458
  (55 shorter events, 9.9 us)
Async XLA Ops:
  7.2 113.3 %all-gather.3.cloned.1.call-start = ((), (), s32[]{:S(2)}) async-start(), calls=%async_computation.5 | async-start | bytes 4456448 | tf_op jit(solution)/shard_map/all_gather | solution.py:386
  10.2 69.6 %copy-start = (f32[4096]{0:T(1024)S(1)}, f32[4096]{0:T(1024)}, u32[]{:S(2)}) copy-start(f32[4096]{0:T(1024)} %param.19) | copy-start | bytes 49156
  64.5 19.1 %collective-permute-start.1 = (bf16[16,64,384]{2,1,0:T(8,128)(2,1)S(1)}, bf16[16,64,384]{2,1,0:T(8,128)(2,1)S(1)}, u32[]{:S(2)}, u32[]{:S(2)}) collective-permute-start(bf16[16,64,384]{2,1,0:T(8,128)(2,1)S(1)} %bitcast.29), channel_id=1, source_target_pairs={{0,24},{8,0},{16,8},{24,16},{1,25},{9,1},{17,9},{25,17},{2,26},{10... | collective-permute-start | bytes 2359304 | tf_op jit(solution)/shard_map/ppermute | solution.py:405
  66.4 22.4 %collective-permute-start = (bf16[16,64,384]{2,1,0:T(8,128)(2,1)S(1)}, bf16[16,64,384]{2,1,0:T(8,128)(2,1)S(1)}, u32[]{:S(2)}, u32[]{:S(2)}) collective-permute-start(bf16[16,64,384]{2,1,0:T(8,128)(2,1)S(1)} %bitcast.30), channel_id=1, source_target_pairs={{0,8},{8,16},{16,24},{24,0},{1,9},{9,17},{17,25},{25,1},{2,10},{10... | collective-permute-start | bytes 2359304 | tf_op jit(solution)/shard_map/ppermute | solution.py:404
  69.7 26.9 %all-to-all-start = ((f32[64,8,128]{2,1,0:T(8,128)}), f32[64,8,128]{2,1,0:T(8,128)S(1)}, u32[]{:S(2)}, u32[]{:S(2)}) async-start(f32[64,8,128]{2,1,0:T(8,128)} %shard_map.242), calls=%async_computation | async-start | bytes 524288 | tf_op jit(solution)/shard_map/all_to_all | solution.py:400
  77.0 2.9 %copy-start.8 = (bf16[1,384,4096]{2,1,0:T(8,128)(2,1)S(1)}, bf16[1,384,4096]{2,1,0:T(8,128)(2,1)}, u32[]{:S(2)}) copy-start(bf16[1,384,4096]{2,1,0:T(8,128)(2,1)} %param.18) | copy-start | bytes 9437188
  83.6 1.0 copy-start.9
  84.6 35.8 %collective-permute-start.3 = (bf16[8,64,384]{2,1,0:T(8,128)(2,1)S(1)}, bf16[8,64,384]{2,1,0:T(8,128)(2,1)S(1)}, u32[]{:S(2)}, u32[]{:S(2)}) collective-permute-start(bf16[8,64,384]{2,1,0:T(8,128)(2,1)S(1)} %slice.46), channel_id=1, source_target_pairs={{0,24},{8,0},{16,8},{24,16},{1,25},{9,1},{17,9},{25,17},{2,26},{10... | collective-permute-start | bytes 1179656 | tf_op jit(solution)/shard_map/ppermute | solution.py:407
  89.6 30.9 %collective-permute-start.2 = (bf16[8,64,384]{2,1,0:T(8,128)(2,1)}, bf16[8,64,384]{2,1,0:T(8,128)(2,1)S(1)}, u32[]{:S(2)}, u32[]{:S(2)}) collective-permute-start(bf16[8,64,384]{2,1,0:T(8,128)(2,1)} %slice.45), channel_id=1, source_target_pairs={{0,8},{8,16},{16,24},{24,0},{1,9},{9,17},{17,25},{25,1},{2,10},{10... | collective-permute-start | bytes 1179656 | tf_op jit(solution)/shard_map/ppermute | solution.py:406
  97.4 23.1 %all-to-all-start.1 = ((f32[8,8,128]{2,1,0:T(8,128)}), f32[8,8,128]{2,1,0:T(8,128)S(1)}, u32[]{:S(2)}, u32[]{:S(2)}) async-start(f32[8,8,128]{2,1,0:T(8,128)} %broadcast_in_dim.7), calls=%async_computation.1 | async-start | bytes 65536 | tf_op jit(solution)/shard_map/all_to_all | solution.py:409
  134.8 47.4 %copy-start.7 = (s32[64]{0:T(128)S(1)}, s32[64]{0:T(128)}, u32[]{:S(2)}) copy-start(s32[64]{0:T(128)} %fusion.6) | copy-start | bytes 772
  134.8 56.8 %copy-start.10 = (f32[64,512]{1,0:T(8,128)S(1)}, f32[64,512]{1,0:T(8,128)}, u32[]{:S(2)}) copy-start(f32[64,512]{1,0:T(8,128)} %col_ref.1) | copy-start | bytes 393220
  134.8 56.7 %copy-start.11 = (f32[64,512]{1,0:T(8,128)S(1)}, f32[64,512]{1,0:T(8,128)}, u32[]{:S(2)}) copy-start(f32[64,512]{1,0:T(8,128)} %param.32) | copy-start | bytes 393220
  134.8 56.7 %copy-start.12 = (f32[64,512]{1,0:T(8,128)S(1)}, f32[64,512]{1,0:T(8,128)}, u32[]{:S(2)}) copy-start(f32[64,512]{1,0:T(8,128)} %param.33) | copy-start | bytes 393220
  134.8 4.3 %collective-permute-start.4 = (bf16[4,16,4224]{2,1,0:T(8,128)(2,1)S(1)}, bf16[4,16,4224]{2,1,0:T(8,128)(2,1)S(1)}, u32[]{:S(2)}, u32[]{:S(2)}) collective-permute-start(bf16[4,16,4224]{2,1,0:T(8,128)(2,1)S(1)} %get-tuple-element.32), channel_id=1, source_target_pairs={{0,1},{1,0},{2,3},{3,2},{4,5},{5,4},{6,7},{7,6},{8,9},{9,8},{10,11... | collective-permute-start | bytes 1622024 | tf_op jit(solution)/shard_map/ppermute | solution.py:436
  139.1 57.3 %copy-start.1 = (f32[100,64]{0,1:T(8,128)S(1)}, f32[100,64]{0,1:T(8,128)}, u32[]{:S(2)}) copy-start(f32[100,64]{0,1:T(8,128)} %param.25) | copy-start | bytes 76804
  139.1 57.3 %copy-start.2 = (f32[64,100]{1,0:T(8,128)S(1)}, f32[64,100]{1,0:T(8,128)}, u32[]{:S(2)}) copy-start(f32[64,100]{1,0:T(8,128)} %refs_1_.3) | copy-start | bytes 76804
  139.1 57.3 %copy-start.3 = (f32[100,64]{0,1:T(8,128)S(1)}, f32[100,64]{0,1:T(8,128)}, u32[]{:S(2)}) copy-start(f32[100,64]{0,1:T(8,128)} %param.26) | copy-start | bytes 76804
  139.1 57.3 %copy-start.4 = (f32[64,100]{1,0:T(8,128)S(1)}, f32[64,100]{1,0:T(8,128)}, u32[]{:S(2)}) copy-start(f32[64,100]{1,0:T(8,128)} %refs_3_.3) | copy-start | bytes 76804
  139.1 57.3 %copy-start.5 = (f32[100,64]{0,1:T(8,128)S(1)}, f32[100,64]{0,1:T(8,128)}, u32[]{:S(2)}) copy-start(f32[100,64]{0,1:T(8,128)} %param.27) | copy-start | bytes 76804
  139.1 57.3 %copy-start.6 = (f32[64,100]{1,0:T(8,128)S(1)}, f32[64,100]{1,0:T(8,128)}, u32[]{:S(2)}) copy-start(f32[64,100]{1,0:T(8,128)} %refs_5_.1) | copy-start | bytes 76804
  183.2 13.2 %all-to-all-start.4 = ((f32[8,16,128]{2,1,0:T(8,128)}), f32[8,16,128]{2,1,0:T(8,128)S(1)}, u32[]{:S(2)}, u32[]{:S(2)}) async-start(f32[8,16,128]{2,1,0:T(8,128)} %get-tuple-element.37), calls=%async_computation.4 | async-start | bytes 131072 | tf_op jit(solution)/shard_map/all_to_all | solution.py:458
Sparse Core Ops, SparseCore 0:
  23.2 88.7 all-gather.2
